TPU v7x, 256 devices: a whole 4x4x8 slice. The times are simulated.
256 devices in a mesh: rows: 256 (over y, x, z, core).
Axes of the slice: x: 4, y: 4, z: 8, core: 2. Of those that a mesh axis runs over, the one named last changes fastest.
Arguments:
- query: bfloat16 [65536, 2048], P('rows'), may hold values from -114 to 114
- response_keys: bfloat16 [65536, 256], P('rows'), may hold values from -6 to 6
- response_values: bfloat16 [65536, 256], P('rows'), may hold values from -6 to 6
- prompt_keys: bfloat16 [32768, 256], P('rows'), may hold values from -6.1 to 6.1
- prompt_values: bfloat16 [32768, 256], P('rows'), may hold values from -6 to 6
- dout: bfloat16 [65536, 2048], P('rows'), may hold values from -6 to 6
- row_slot: int32 [65536], P('rows'), may hold values from -1 to 3, as said below
- row_pos: int32 [65536], P('rows'), may hold values from 0 to 255, as said below
Outputs:
- attended_out: bfloat16 [65536, 2048], P('rows')
- grad_query: bfloat16 [65536, 2048], P('rows')
- grad_response_keys: bfloat16 [65536, 256], P('rows')
- grad_response_values: bfloat16 [65536, 256], P('rows')
- grad_prompt_keys: bfloat16 [32768, 256], P('rows')
- grad_prompt_values: bfloat16 [32768, 256], P('rows')
Inputs may be any that keep to these rules, and one draw needn't show every extreme that they name: `row_slot`: every response of a prompt lies whole, in consecutive rows and positions 0, 1, 2 and so on, on one device of that prompt's 4 devices; a prompt has 4 responses of 64 to 256 rows each, and in every group some device is filled by one response of 256 rows. Other rows are empty. `row_pos`: 0 on empty rows.
All inputs are finite; a program needn't handle non-finite values.
Results may differ from a plain program's by a relative error of at most 0.0065.
Values may be sent and summed in bfloat16 or wider, within the bound.
No kernel may reach another device: no remote copies, remote signals or barrier semaphores. Data moves between devices by JAX's collectives and lax.ppermute only.
A program may use at most 128 MiB of HBM per device.

v0:
```python
import jax
import jax.numpy as jnp
from jax import lax
from jax.sharding import PartitionSpec as P

QUERY_HEADS = 16
KV_HEADS = 2
HEAD_DIM = 128
GROUP = 4


def shifted(block, axis, distance):
    devices = range(lax.axis_size(axis))
    route = [(i - distance, i) for i in devices if i - distance in devices]
    return lax.ppermute(block, axis, route)


def head_pass(query_rows, grad_rows, key_rows, value_rows, allowed, group_heads):
    row_count = allowed.shape[0]
    scores = jnp.dot(query_rows, key_rows.T, preferred_element_type=jnp.float32) * HEAD_DIM ** (
        -0.5
    )
    scores = scores.reshape(row_count, group_heads, -1)
    scores = jnp.where(allowed[:, None, :], scores, jnp.float32(-1e30))
    scores = scores.reshape(row_count * group_heads, -1)
    biggest = jnp.max(scores, axis=1, keepdims=True)
    weights = jnp.exp(scores - biggest)
    weights = weights / jnp.sum(weights, axis=1, keepdims=True)
    weights_low = weights.astype(jnp.bfloat16)
    attended = jnp.dot(weights_low, value_rows, preferred_element_type=jnp.float32)
    pressure = jnp.dot(grad_rows, value_rows.T, preferred_element_type=jnp.float32)
    centre = jnp.sum(weights * pressure, axis=1, keepdims=True)
    slopes = (weights * (pressure - centre) * HEAD_DIM ** (-0.5)).astype(jnp.bfloat16)
    grad_q = jnp.dot(slopes, key_rows, preferred_element_type=jnp.float32)
    grad_k = jnp.dot(slopes.T, query_rows, preferred_element_type=jnp.float32)
    grad_v = jnp.dot(weights_low.T, grad_rows, preferred_element_type=jnp.float32)
    return (attended, grad_q, grad_k, grad_v)


def device_block(
    query, response_keys, response_values, prompt_keys, prompt_values, dout, row_slot, row_pos
):
    row_count = query.shape[0]
    prompt_rows = prompt_keys.shape[0]
    live_rows = row_slot >= 0
    same_resp = (
        (row_slot[:, None] == row_slot[None, :])
        & live_rows[None, :]
        & (row_pos[None, :] <= row_pos[:, None])
    )
    allowed = jnp.concatenate([jnp.ones((row_count, prompt_rows), dtype=bool), same_resp], axis=1)
    grad_live = jnp.where(live_rows[:, None], dout, jnp.zeros_like(dout))
    all_keys = jnp.concatenate([prompt_keys, response_keys], axis=0)
    all_values = jnp.concatenate([prompt_values, response_values], axis=0)
    group_heads = QUERY_HEADS // KV_HEADS
    width_cols = group_heads * HEAD_DIM
    outs_list, dq_list, dk_list, dv_list = ([], [], [], [])
    for kv_head in range(KV_HEADS):
        query_cols = query[:, kv_head * width_cols : (kv_head + 1) * width_cols].reshape(
            row_count * group_heads, HEAD_DIM
        )
        grad_cols = grad_live[:, kv_head * width_cols : (kv_head + 1) * width_cols].reshape(
            row_count * group_heads, HEAD_DIM
        )
        key_cols = all_keys[:, kv_head * HEAD_DIM : (kv_head + 1) * HEAD_DIM]
        value_cols = all_values[:, kv_head * HEAD_DIM : (kv_head + 1) * HEAD_DIM]
        attended, grad_q, grad_k, grad_v = head_pass(
            query_cols, grad_cols, key_cols, value_cols, allowed, group_heads
        )
        outs_list.append(attended.reshape(row_count, width_cols))
        dq_list.append(grad_q.reshape(row_count, width_cols))
        dk_list.append(grad_k)
        dv_list.append(grad_v)
    outputs = jnp.concatenate(outs_list, axis=1)
    outputs = jnp.where(live_rows[:, None], outputs, jnp.zeros_like(outputs)).astype(jnp.bfloat16)
    grad_query = jnp.concatenate(dq_list, axis=1).astype(jnp.bfloat16)
    key_terms = jnp.concatenate(dk_list, axis=1)
    value_terms = jnp.concatenate(dv_list, axis=1)
    return (
        outputs,
        grad_query,
        key_terms[prompt_rows:].astype(jnp.bfloat16),
        value_terms[prompt_rows:].astype(jnp.bfloat16),
        key_terms[:prompt_rows].astype(jnp.bfloat16),
        value_terms[:prompt_rows].astype(jnp.bfloat16),
    )


def per_device(
    query, response_keys, response_values, prompt_keys, prompt_values, dout, row_slot, row_pos
):
    shard_rows = prompt_keys.shape[0]
    stride = lax.axis_size("rows") // GROUP
    member = lax.axis_index("rows") // stride
    stacked = jnp.stack([prompt_keys, prompt_values])
    lower_side = []
    upper_side = []
    for offset in range(1, GROUP):
        lower_side.append(shifted(stacked, "rows", offset * stride))
        upper_side.append(shifted(stacked, "rows", -offset * stride))
    relative = jnp.stack(list(reversed(lower_side)) + [stacked] + upper_side)
    shards = []
    for owner in range(GROUP):
        picked = lax.dynamic_index_in_dim(relative, owner - member + GROUP - 1, 0, keepdims=False)
        shards.append(picked)
    gathered = jnp.concatenate(shards, axis=1)
    results = device_block(
        query, response_keys, response_values, gathered[0], gathered[1], dout, row_slot, row_pos
    )
    partials = jnp.stack([results[4], results[5]])
    summed = lax.dynamic_slice_in_dim(partials, member * shard_rows, shard_rows, 1).astype(
        jnp.float32
    )
    for offset in range(1, GROUP):
        target_up = member + offset
        portion = lax.dynamic_slice_in_dim(
            partials, jnp.minimum(target_up, GROUP - 1) * shard_rows, shard_rows, 1
        )
        portion = jnp.where(target_up < GROUP, portion, jnp.zeros_like(portion))
        summed = summed + shifted(portion, "rows", offset * stride).astype(jnp.float32)
        target_down = member - offset
        portion = lax.dynamic_slice_in_dim(
            partials, jnp.maximum(target_down, 0) * shard_rows, shard_rows, 1
        )
        portion = jnp.where(target_down >= 0, portion, jnp.zeros_like(portion))
        summed = summed + shifted(portion, "rows", -offset * stride).astype(jnp.float32)
    return (
        results[0],
        results[1],
        results[2],
        results[3],
        summed[0].astype(jnp.bfloat16),
        summed[1].astype(jnp.bfloat16),
    )


def solution(mesh):
    in_specs = (
        P("rows", None),
        P("rows", None),
        P("rows", None),
        P("rows", None),
        P("rows", None),
        P("rows", None),
        P("rows"),
        P("rows"),
    )
    out_specs = (
        P("rows", None),
        P("rows", None),
        P("rows", None),
        P("rows", None),
        P("rows", None),
        P("rows", None),
    )
    return jax.shard_map(
        per_device, mesh=mesh, in_specs=in_specs, out_specs=out_specs, check_vma=False
    )
```

profile of v0, /device:TPU:96, one launch (start us, length us, event | category | flops | bytes accessed | tf_op | source)
XLA Modules:
  0.0 117.6 jit_solution(7982783481815574282)
XLA Ops:
  0.6 1.5 %pad_maximum_fusion.6 = bf16[2,128,256]{2,1,0:T(8,128)(2,1)} fusion(bf16[1,128,256]{2,1,0:T(8,128)(2,1)} %bitcast.62, bf16[1,128,256]{2,1,0:T(8,128)(2,1)} %bitcast.64), kind=kLoop, calls=%fused_computation.75 | loop fusion | flops 65536 | bytes 262144 | tf_op jit(solution)/shard_map/stack | solution.py:95
  2.2 5.6 %collective-permute-start = (bf16[2,128,256]{2,1,0:T(8,128)(2,1)}, bf16[2,128,256]{2,1,0:T(8,128)(2,1)}, u32[]{:S(2)}, u32[]{:S(2)}) collective-permute-start(bf16[2,128,256]{2,1,0:T(8,128)(2,1)} %pad_maximum_fusion.6), channel_id=1, source_target_pairs={{0,192},{1,193},{2,194},{3,195},{4,196},{5,197},{6,198},{7,199},{8... | collective-permute-start | bytes 393224 | tf_op jit(solution)/shard_map/ppermute | solution.py:15
  7.7 1.9 %collective-permute-start.1 = (bf16[2,128,256]{2,1,0:T(8,128)(2,1)}, bf16[2,128,256]{2,1,0:T(8,128)(2,1)}, u32[]{:S(2)}, u32[]{:S(2)}) collective-permute-start(bf16[2,128,256]{2,1,0:T(8,128)(2,1)} %pad_maximum_fusion.6), channel_id=1, source_target_pairs={{0,128},{1,129},{2,130},{3,131},{4,132},{5,133},{6,134},{7,135},{8... | collective-permute-start | bytes 393224 | tf_op jit(solution)/shard_map/ppermute | solution.py:15
  9.7 2.8 %collective-permute-start.2 = (bf16[2,128,256]{2,1,0:T(8,128)(2,1)}, bf16[2,128,256]{2,1,0:T(8,128)(2,1)}, u32[]{:S(2)}, u32[]{:S(2)}) collective-permute-start(bf16[2,128,256]{2,1,0:T(8,128)(2,1)} %pad_maximum_fusion.6), channel_id=1, source_target_pairs={{0,64},{1,65},{2,66},{3,67},{4,68},{5,69},{6,70},{7,71},{8,72},{9,... | collective-permute-start | bytes 393224 | tf_op jit(solution)/shard_map/ppermute | solution.py:15
  12.4 1.3 %collective-permute-start.3 = (bf16[2,128,256]{2,1,0:T(8,128)(2,1)}, bf16[2,128,256]{2,1,0:T(8,128)(2,1)}, u32[]{:S(2)}, u32[]{:S(2)}) collective-permute-start(bf16[2,128,256]{2,1,0:T(8,128)(2,1)} %pad_maximum_fusion.6), channel_id=1, source_target_pairs={{64,0},{65,1},{66,2},{67,3},{68,4},{69,5},{70,6},{71,7},{72,8},{73... | collective-permute-start | bytes 393224 | tf_op jit(solution)/shard_map/ppermute | solution.py:15
  13.7 1.3 %collective-permute-start.4 = (bf16[2,128,256]{2,1,0:T(8,128)(2,1)}, bf16[2,128,256]{2,1,0:T(8,128)(2,1)}, u32[]{:S(2)}, u32[]{:S(2)}) collective-permute-start(bf16[2,128,256]{2,1,0:T(8,128)(2,1)} %pad_maximum_fusion.6), channel_id=1, source_target_pairs={{128,0},{129,1},{130,2},{131,3},{132,4},{133,5},{134,6},{135,7},{1... | collective-permute-start | bytes 393224 | tf_op jit(solution)/shard_map/ppermute | solution.py:15
  15.0 0.7 broadcast_compare_fusion
  15.7 0.9 compare_and_fusion
  16.7 0.7 broadcast_bitcast_fusion
  17.4 2.3 %fusion.47 = (bf16[256,1024]{1,0:T(8,128)(2,1)}, bf16[256,1024]{1,0:T(8,128)(2,1)}) fusion(bf16[256,2048]{1,0:T(8,128)(2,1)} %param.8), kind=kLoop, calls=%fused_computation.97 | loop fusion | bytes 2097152 | tf_op jit(solution)/shard_map/slice | solution.py:59
  19.7 1.7 %copy.18 = pred[2048,768]{0,1:T(32,128)(4,1)S(1)} copy(pred[2048,768]{1,0:T(32,128)(4,1)S(1)} %broadcast_bitcast_fusion) | data formatting | bytes 3145728 | tf_op jit(solution)/shard_map/jit(_where)/broadcast_in_dim | solution.py:24
  21.4 1.3 %reshape.59 = bf16[2048,128]{1,0:T(8,128)(2,1)S(1)} reshape(bf16[256,1024]{1,0:T(8,128)(2,1)} %get-tuple-element.20) | data formatting | bytes 1048576 | tf_op jit(solution)/shard_map/reshape | solution.py:59
  22.7 1.3 %reshape.61 = bf16[2048,128]{1,0:T(8,128)(2,1)S(1)} reshape(bf16[256,1024]{1,0:T(8,128)(2,1)} %get-tuple-element.21) | data formatting | bytes 1048576 | tf_op jit(solution)/shard_map/reshape | solution.py:59
  24.0 1.5 %collective-permute-start.5 = (bf16[2,128,256]{2,1,0:T(8,128)(2,1)}, bf16[2,128,256]{2,1,0:T(8,128)(2,1)S(1)}, u32[]{:S(2)}, u32[]{:S(2)}) collective-permute-start(bf16[2,128,256]{2,1,0:T(8,128)(2,1)} %pad_maximum_fusion.6), channel_id=1, source_target_pairs={{192,0},{193,1},{194,2},{195,3},{196,4},{197,5},{198,6},{199,7},{2... | collective-permute-start | bytes 393224 | tf_op jit(solution)/shard_map/ppermute | solution.py:15
  25.5 0.9 bitcast_dynamic-update-slice_fusion.6
  26.4 0.9 bitcast_dynamic-update-slice_fusion.5
  27.4 0.9 bitcast_dynamic-update-slice_fusion.4
  28.3 0.9 bitcast_dynamic-update-slice_fusion.3
  29.2 0.9 bitcast_dynamic-update-slice_fusion.2
  30.1 0.9 bitcast_dynamic-update-slice_fusion.1
  31.0 4.0 %collective-permute-done.5 = bf16[2,128,256]{2,1,0:T(8,128)(2,1)S(1)} collective-permute-done((bf16[2,128,256]{2,1,0:T(8,128)(2,1)}, bf16[2,128,256]{2,1,0:T(8,128)(2,1)S(1)}, u32[]{:S(2)}, u32[]{:S(2)}) %collective-permute-start.5) | collective-permute-done | bytes 131104 | tf_op jit(solution)/shard_map/ppermute | solution.py:15
  35.2 1.3 %fusion.49 = (f32[2048]{0:T(1024)S(1)}, f32[2048,768]{0,1:T(8,128)S(1)}) fusion(pred[2048,768]{0,1:T(32,128)(4,1)S(1)} %copy.18, bf16[2048,128]{1,0:T(8,128)(2,1)S(1)} %reshape.59, bf16[512,256]{1,0:T(8,128)(2,1)S(1)} %get-tuple-element.32, bf16[256,256]{1,0:T(8,128)(2,1)S(1)} %copy-done.2), kind=kOutput, calls=%fused_computation.99 | convolution fusion | flops 407762944 | bytes 8790016 | tf_op jit(solution)/shard_map/dot_general | solution.py:20
  36.5 0.9 fusion.1
  37.4 1.8 %copy-done.1 = f32[2048,768]{0,1:T(8,128)} copy-done((f32[2048,768]{0,1:T(8,128)}, f32[2048,768]{0,1:T(8,128)S(1)}, u32[]{:S(2)}) %copy-start.1) | copy-done | bytes 6291480
  39.2 2.1 %fusion.11 = bf16[2048,128]{1,0:T(8,128)(2,1)} fusion(bf16[512,256]{1,0:T(8,128)(2,1)S(1)} %get-tuple-element.33, bf16[256,256]{1,0:T(8,128)(2,1)S(1)} %copy-done.19, f32[2048,768]{0,1:T(8,128)S(1)} %get-tuple-element.41, f32[2048]{0:T(1024)S(1)} %fusion.1, f32[2048]{0:T(1024)S(1)} %get-tuple-element.40), kind=kOutput, calls=%fused_computation.23 | convolution fusion | flops 407764992 | bytes 7225344 | tf_op jit(solution)/shard_map/dot_general | solution.py:30
  41.3 1.3 %reshape.60 = bf16[256,1024]{1,0:T(8,128)(2,1)S(1)} reshape(bf16[2048,128]{1,0:T(8,128)(2,1)} %fusion.11) | data formatting | bytes 1048576 | tf_op jit(solution)/shard_map/reshape | solution.py:70
  42.6 1.3 %fusion.48 = (f32[2048]{0:T(1024)S(1)}, f32[2048,768]{0,1:T(8,128)S(1)}) fusion(pred[2048,768]{0,1:T(32,128)(4,1)S(1)} %copy.18, bf16[2048,128]{1,0:T(8,128)(2,1)S(1)} %reshape.61, bf16[256,256]{1,0:T(8,128)(2,1)S(1)} %copy-done.2, bf16[512,256]{1,0:T(8,128)(2,1)S(1)} %get-tuple-element.32), kind=kOutput, calls=%fused_computation.98 | convolution fusion | flops 407762944 | bytes 8790016 | tf_op jit(solution)/shard_map/dot_general | solution.py:20
  43.9 0.9 fusion.3
  44.8 1.8 %copy-done = f32[2048,768]{0,1:T(8,128)} copy-done((f32[2048,768]{0,1:T(8,128)}, f32[2048,768]{0,1:T(8,128)S(1)}, u32[]{:S(2)}) %copy-start) | copy-done | bytes 6291480
  46.6 0.6 copy-done.12
  47.2 2.1 %fusion.7 = bf16[2048,128]{1,0:T(8,128)(2,1)} fusion(bf16[256,256]{1,0:T(8,128)(2,1)S(1)} %copy-done.20, bf16[512,256]{1,0:T(8,128)(2,1)S(1)} %copy-done.9, f32[2048,768]{0,1:T(8,128)S(1)} %get-tuple-element.39, f32[2048]{0:T(1024)S(1)} %fusion.3, f32[2048]{0:T(1024)S(1)} %get-tuple-element.38), kind=kOutput, calls=%fused_computation.19 | convolution fusion | flops 407764992 | bytes 7225344 | tf_op jit(solution)/shard_map/dot_general | solution.py:30
  49.3 1.3 %reshape.62 = bf16[256,1024]{1,0:T(8,128)(2,1)S(1)} reshape(bf16[2048,128]{1,0:T(8,128)(2,1)} %fusion.7) | data formatting | bytes 1048576 | tf_op jit(solution)/shard_map/reshape | solution.py:70
  50.6 2.2 %broadcast_select_fusion = (bf16[256,2048]{1,0:T(8,128)(2,1)S(1)}, bf16[256,2048]{1,0:T(8,128)(2,1)}) fusion(bf16[256,2048]{1,0:T(8,128)(2,1)S(1)} %copy-done.4, pred[256]{0:T(512)(128)(4,1)} %copy-done.18, bf16[256,1024]{1,0:T(8,128)(2,1)S(1)} %reshape.62, bf16[256,1024]{1,0:T(8,128)(2,1)S(1)} %reshape.60), kind=kLoop, calls=%fused_computation.26 | loop fusion | flops 3145728 | bytes 4194560 | tf_op jit(solution)/shard_map/jit(_where)/select_n | solution.py:52
  52.8 1.0 fusion.46
  53.8 2.2 %reshape.63 = bf16[2048,128]{1,0:T(8,128)(2,1)} reshape(bf16[256,1024]{1,0:T(8,128)(2,1)} %get-tuple-element.18) | data formatting | bytes 1048576 | tf_op jit(solution)/shard_map/reshape | solution.py:62
  56.1 5.1 %fusion.9 = bf16[768,128]{0,1:T(8,128)(2,1)} fusion(bf16[2048,128]{1,0:T(8,128)(2,1)} %reshape.63, f32[2048,768]{0,1:T(8,128)} %copy-done.1, f32[2048]{0:T(1024)} %copy-done.14, f32[2048]{0:T(1024)S(1)} %get-tuple-element.40), kind=kOutput, calls=%fused_computation.21 | convolution fusion | flops 407371776 | bytes 7028736 | tf_op jit(solution)/shard_map/dot_general | solution.py:36
  61.2 4.4 %multiply_reduce_fusion.1 = (f32[2048]{0:T(1024)}, f32[2048,768]{0,1:T(8,128)}) fusion(f32[2048]{0:T(1024)S(1)} %copy-done.15, f32[2048,768]{0,1:T(8,128)S(1)} %bitcast.57, f32[2048]{0:T(1024)S(1)} %get-tuple-element.40, bf16[2048,128]{1,0:T(8,128)(2,1)S(1)} %copy-done.7, bf16[512,256]{1,0:T(8,128)(2,1)S(1)} %copy-done.10, bf16[256,256]{1,0:T(8,128)(2,1)S(1)} %copy-done.21), kind=kOutput, calls=%fused_computation.5 | convolution fusion | flops 409335808 | bytes 13524992 | tf_op jit(solution)/shard_map/dot_general | solution.py:31
  65.6 2.2 %reshape.65 = bf16[2048,128]{1,0:T(8,128)(2,1)} reshape(bf16[256,1024]{1,0:T(8,128)(2,1)} %get-tuple-element.19) | data formatting | bytes 1048576 | tf_op jit(solution)/shard_map/reshape | solution.py:62
  67.9 4.4 %fusion.5 = bf16[768,128]{0,1:T(8,128)(2,1)S(1)} fusion(bf16[2048,128]{1,0:T(8,128)(2,1)} %reshape.65, f32[2048,768]{0,1:T(8,128)} %copy-done, f32[2048]{0:T(1024)} %copy-done.12, f32[2048]{0:T(1024)S(1)} %get-tuple-element.38), kind=kOutput, calls=%fused_computation.17 | convolution fusion | flops 407371776 | bytes 7028736 | tf_op jit(solution)/shard_map/dot_general | solution.py:36
  72.4 1.4 %multiply_reduce_fusion = (f32[2048]{0:T(1024)S(1)}, f32[2048,768]{0,1:T(8,128)S(1)}) fusion(f32[2048]{0:T(1024)S(1)} %copy-done.13, f32[2048,768]{0,1:T(8,128)S(1)} %bitcast.55, f32[2048]{0:T(1024)S(1)} %get-tuple-element.38, bf16[2048,128]{1,0:T(8,128)(2,1)S(1)} %copy-done.6, bf16[256,256]{1,0:T(8,128)(2,1)S(1)} %copy-done.22, ...), kind=kOutput, calls=%fused_computation.3 | convolution fusion | flops 409335808 | bytes 13524992 | tf_op jit(solution)/shard_map/dot_general | solution.py:31
  73.8 1.0 slice-done.6
  74.8 0.8 slice-done.5
  75.6 0.6 slice-done.7
  76.2 1.8 %multiply_convert_fusion.1 = bf16[2048,768]{0,1:T(8,128)(2,1)S(1)} fusion(f32[2048,768]{0,1:T(8,128)S(1)} %bitcast.61, f32[2048]{0:T(1024)S(1)} %copy-done.17, f32[2048]{0:T(1024)S(1)} %copy-done.16, f32[2048,768]{0,1:T(8,128)S(1)} %bitcast.59, f32[2048]{0:T(1024)S(1)} %get-tuple-element.40), kind=kLoop, calls=%fused_computation.4 | loop fusion | flops 9437184 | bytes 15753216 | tf_op jit(solution)/shard_map/convert_element_type | solution.py:33
  77.9 1.2 fusion.50
  79.1 1.0 convolution_convert_fusion.1
  80.2 1.7 %multiply_convert_fusion = bf16[2048,768]{0,1:T(8,128)(2,1)S(1)} fusion(f32[2048,768]{0,1:T(8,128)S(1)} %get-tuple-element.43, f32[2048]{0:T(1024)S(1)} %get-tuple-element.42, f32[2048]{0:T(1024)S(1)} %copy-done.13, f32[2048,768]{0,1:T(8,128)S(1)} %bitcast.55, f32[2048]{0:T(1024)S(1)} %get-tuple-element.38), kind=kLoop, calls=%fused_computation.2 | loop fusion | flops 9437184 | bytes 15753216 | tf_op jit(solution)/shard_map/convert_element_type | solution.py:33
  81.9 1.2 fusion.51
  83.1 1.0 convolution_convert_fusion
  84.2 0.8 fusion.23
  85.0 1.3 %collective-permute-start.6 = (bf16[2,128,256]{1,2,0:T(8,128)(2,1)}, bf16[2,128,256]{1,2,0:T(8,128)(2,1)S(1)}, u32[]{:S(2)}, u32[]{:S(2)}) collective-permute-start(bf16[2,128,256]{1,2,0:T(8,128)(2,1)} %get-tuple-element.26), channel_id=1, source_target_pairs={{0,64},{1,65},{2,66},{3,67},{4,68},{5,69},{6,70},{7,71},{8,72},{9,... | collective-permute-start | bytes 393224 | tf_op jit(solution)/shard_map/ppermute | solution.py:15
  86.3 1.3 %collective-permute-start.7 = (bf16[2,128,256]{1,2,0:T(8,128)(2,1)}, bf16[2,128,256]{1,2,0:T(8,128)(2,1)S(1)}, u32[]{:S(2)}, u32[]{:S(2)}) collective-permute-start(bf16[2,128,256]{1,2,0:T(8,128)(2,1)} %get-tuple-element.27), channel_id=1, source_target_pairs={{64,0},{65,1},{66,2},{67,3},{68,4},{69,5},{70,6},{71,7},{72,8},{73... | collective-permute-start | bytes 393224 | tf_op jit(solution)/shard_map/ppermute | solution.py:15
  87.6 7.2 %collective-permute-start.8 = (bf16[2,128,256]{1,2,0:T(8,128)(2,1)S(1)}, bf16[2,128,256]{1,2,0:T(8,128)(2,1)S(1)}, u32[]{:S(2)}, u32[]{:S(2)}) collective-permute-start(bf16[2,128,256]{1,2,0:T(8,128)(2,1)S(1)} %get-tuple-element.28), channel_id=1, source_target_pairs={{0,128},{1,129},{2,130},{3,131},{4,132},{5,133},{6,134},{7,135},{8... | collective-permute-start | bytes 393224 | tf_op jit(solution)/shard_map/ppermute | solution.py:15
  94.9 1.3 %collective-permute-start.9 = (bf16[2,128,256]{1,2,0:T(8,128)(2,1)S(1)}, bf16[2,128,256]{1,2,0:T(8,128)(2,1)}, u32[]{:S(2)}, u32[]{:S(2)}) collective-permute-start(bf16[2,128,256]{1,2,0:T(8,128)(2,1)S(1)} %get-tuple-element.29), channel_id=1, source_target_pairs={{128,0},{129,1},{130,2},{131,3},{132,4},{133,5},{134,6},{135,7},{1... | collective-permute-start | bytes 393224 | tf_op jit(solution)/shard_map/ppermute | solution.py:15
  96.2 7.9 %collective-permute-start.10 = (bf16[2,128,256]{1,2,0:T(8,128)(2,1)S(1)}, bf16[2,128,256]{1,2,0:T(8,128)(2,1)}, u32[]{:S(2)}, u32[]{:S(2)}) collective-permute-start(bf16[2,128,256]{1,2,0:T(8,128)(2,1)S(1)} %get-tuple-element.30), channel_id=1, source_target_pairs={{0,192},{1,193},{2,194},{3,195},{4,196},{5,197},{6,198},{7,199},{8... | collective-permute-start | bytes 393224 | tf_op jit(solution)/shard_map/ppermute | solution.py:15
  104.1 0.8 copy.21
  104.9 0.8 maximum_convert_fusion.1
  105.7 0.8 copy.20
  107.0 1.3 %collective-permute-start.11 = (bf16[2,128,256]{1,2,0:T(8,128)(2,1)S(1)}, bf16[2,128,256]{1,2,0:T(8,128)(2,1)S(1)}, u32[]{:S(2)}, u32[]{:S(2)}) collective-permute-start(bf16[2,128,256]{1,2,0:T(8,128)(2,1)S(1)} %get-tuple-element.31), channel_id=1, source_target_pairs={{192,0},{193,1},{194,2},{195,3},{196,4},{197,5},{198,6},{199,7},{2... | collective-permute-start | bytes 393224 | tf_op jit(solution)/shard_map/ppermute | solution.py:15
  108.3 1.1 pad_maximum_fusion
  109.3 5.7 %collective-permute-done.11 = bf16[2,128,256]{1,2,0:T(8,128)(2,1)S(1)} collective-permute-done((bf16[2,128,256]{1,2,0:T(8,128)(2,1)S(1)}, bf16[2,128,256]{1,2,0:T(8,128)(2,1)S(1)}, u32[]{:S(2)}, u32[]{:S(2)}) %collective-permute-start.11) | collective-permute-done | bytes 131104 | tf_op jit(solution)/shard_map/ppermute | solution.py:15
  115.0 1.1 add_convert_fusion
  116.2 0.7 copy.22
  116.9 0.7 copy.23
  (81 shorter events, 0.9 us)
Async XLA Ops:
  2.2 21.8 %collective-permute-start = (bf16[2,128,256]{2,1,0:T(8,128)(2,1)}, bf16[2,128,256]{2,1,0:T(8,128)(2,1)}, u32[]{:S(2)}, u32[]{:S(2)}) collective-permute-start(bf16[2,128,256]{2,1,0:T(8,128)(2,1)} %pad_maximum_fusion.6), channel_id=1, source_target_pairs={{0,192},{1,193},{2,194},{3,195},{4,196},{5,197},{6,198},{7,199},{8... | collective-permute-start | bytes 393224 | tf_op jit(solution)/shard_map/ppermute | solution.py:15
  7.7 18.7 %collective-permute-start.1 = (bf16[2,128,256]{2,1,0:T(8,128)(2,1)}, bf16[2,128,256]{2,1,0:T(8,128)(2,1)}, u32[]{:S(2)}, u32[]{:S(2)}) collective-permute-start(bf16[2,128,256]{2,1,0:T(8,128)(2,1)} %pad_maximum_fusion.6), channel_id=1, source_target_pairs={{0,128},{1,129},{2,130},{3,131},{4,132},{5,133},{6,134},{7,135},{8... | collective-permute-start | bytes 393224 | tf_op jit(solution)/shard_map/ppermute | solution.py:15
  9.7 17.7 %collective-permute-start.2 = (bf16[2,128,256]{2,1,0:T(8,128)(2,1)}, bf16[2,128,256]{2,1,0:T(8,128)(2,1)}, u32[]{:S(2)}, u32[]{:S(2)}) collective-permute-start(bf16[2,128,256]{2,1,0:T(8,128)(2,1)} %pad_maximum_fusion.6), channel_id=1, source_target_pairs={{0,64},{1,65},{2,66},{3,67},{4,68},{5,69},{6,70},{7,71},{8,72},{9,... | collective-permute-start | bytes 393224 | tf_op jit(solution)/shard_map/ppermute | solution.py:15
  12.4 16.7 %collective-permute-start.3 = (bf16[2,128,256]{2,1,0:T(8,128)(2,1)}, bf16[2,128,256]{2,1,0:T(8,128)(2,1)}, u32[]{:S(2)}, u32[]{:S(2)}) collective-permute-start(bf16[2,128,256]{2,1,0:T(8,128)(2,1)} %pad_maximum_fusion.6), channel_id=1, source_target_pairs={{64,0},{65,1},{66,2},{67,3},{68,4},{69,5},{70,6},{71,7},{72,8},{73... | collective-permute-start | bytes 393224 | tf_op jit(solution)/shard_map/ppermute | solution.py:15
  13.7 16.4 %collective-permute-start.4 = (bf16[2,128,256]{2,1,0:T(8,128)(2,1)}, bf16[2,128,256]{2,1,0:T(8,128)(2,1)}, u32[]{:S(2)}, u32[]{:S(2)}) collective-permute-start(bf16[2,128,256]{2,1,0:T(8,128)(2,1)} %pad_maximum_fusion.6), channel_id=1, source_target_pairs={{128,0},{129,1},{130,2},{131,3},{132,4},{133,5},{134,6},{135,7},{1... | collective-permute-start | bytes 393224 | tf_op jit(solution)/shard_map/ppermute | solution.py:15
  15.7 0.9 copy-start.18
  17.4 17.8 %copy-start.2 = (bf16[256,256]{1,0:T(8,128)(2,1)S(1)}, bf16[256,256]{1,0:T(8,128)(2,1)}, u32[]{:S(2)}) copy-start(bf16[256,256]{1,0:T(8,128)(2,1)} %param.9) | copy-start | bytes 393220
  24.0 11.0 %collective-permute-start.5 = (bf16[2,128,256]{2,1,0:T(8,128)(2,1)}, bf16[2,128,256]{2,1,0:T(8,128)(2,1)S(1)}, u32[]{:S(2)}, u32[]{:S(2)}) collective-permute-start(bf16[2,128,256]{2,1,0:T(8,128)(2,1)} %pad_maximum_fusion.6), channel_id=1, source_target_pairs={{192,0},{193,1},{194,2},{195,3},{196,4},{197,5},{198,6},{199,7},{2... | collective-permute-start | bytes 393224 | tf_op jit(solution)/shard_map/ppermute | solution.py:15
  35.2 2.2 %copy-start.8 = (bf16[512,256]{1,0:T(8,128)(2,1)}, bf16[512,256]{1,0:T(8,128)(2,1)S(1)}, u32[]{:S(2)}) copy-start(bf16[512,256]{1,0:T(8,128)(2,1)S(1)} %get-tuple-element.33) | copy-start | bytes 786436
  35.2 4.0 %copy-start.19 = (bf16[256,256]{1,0:T(8,128)(2,1)S(1)}, bf16[256,256]{1,0:T(8,128)(2,1)}, u32[]{:S(2)}) copy-start(bf16[256,256]{1,0:T(8,128)(2,1)} %param.10) | copy-start | bytes 393220
  36.5 2.7 %copy-start.1 = (f32[2048,768]{0,1:T(8,128)}, f32[2048,768]{0,1:T(8,128)S(1)}, u32[]{:S(2)}) copy-start(f32[2048,768]{0,1:T(8,128)S(1)} %get-tuple-element.41) | copy-start | bytes 18874372
  37.4 3.9 %copy-start.14 = (f32[2048]{0:T(1024)}, f32[2048]{0:T(1024)S(1)}, u32[]{:S(2)}) copy-start(f32[2048]{0:T(1024)S(1)} %fusion.1) | copy-start | bytes 24580
  42.6 4.6 %copy-start.9 = (bf16[512,256]{1,0:T(8,128)(2,1)S(1)}, bf16[512,256]{1,0:T(8,128)(2,1)}, u32[]{:S(2)}) copy-start(bf16[512,256]{1,0:T(8,128)(2,1)} %copy-done.8) | copy-start | bytes 786436
  42.6 4.6 %copy-start.20 = (bf16[256,256]{1,0:T(8,128)(2,1)S(1)}, bf16[256,256]{1,0:T(8,128)(2,1)}, u32[]{:S(2)}) copy-start(bf16[256,256]{1,0:T(8,128)(2,1)} %param.10) | copy-start | bytes 393220
  43.9 2.7 %copy-start = (f32[2048,768]{0,1:T(8,128)}, f32[2048,768]{0,1:T(8,128)S(1)}, u32[]{:S(2)}) copy-start(f32[2048,768]{0,1:T(8,128)S(1)} %get-tuple-element.39) | copy-start | bytes 18874372
  46.6 0.6 copy-start.12
  47.2 3.4 %copy-start.4 = (bf16[256,2048]{1,0:T(8,128)(2,1)S(1)}, bf16[256,2048]{1,0:T(8,128)(2,1)}, u32[]{:S(2)}) copy-start(bf16[256,2048]{1,0:T(8,128)(2,1)} %param.13) | copy-start | bytes 3145732
  53.8 7.3 %slice-start.2 = ((s8[6291456]{0:T(1024)(128)(4,1)}), s8[2097152]{0:T(1024)(128)(4,1)S(1)}, s32[]{:S(2)}) async-start(s8[6291456]{0:T(1024)(128)(4,1)} %bitcast.56), calls=%async_computation.2 | async-start | bytes 4194304
  56.1 5.1 %slice-start.3 = ((s8[6291456]{0:T(1024)(128)(4,1)}), s8[4194304]{0:T(1024)(128)(4,1)S(1)}, s32[]{:S(2)}) async-start(s8[6291456]{0:T(1024)(128)(4,1)} %bitcast.56), calls=%async_computation.3 | async-start | bytes 8388608
  56.1 5.1 %copy-start.7 = (bf16[2048,128]{1,0:T(8,128)(2,1)S(1)}, bf16[2048,128]{1,0:T(8,128)(2,1)}, u32[]{:S(2)}) copy-start(bf16[2048,128]{1,0:T(8,128)(2,1)} %reshape.63) | copy-start | bytes 1572868
  56.1 5.1 %copy-start.10 = (bf16[512,256]{1,0:T(8,128)(2,1)S(1)}, bf16[512,256]{1,0:T(8,128)(2,1)}, u32[]{:S(2)}) copy-start(bf16[512,256]{1,0:T(8,128)(2,1)} %copy-done.8) | copy-start | bytes 786436
  56.1 5.1 %copy-start.15 = (f32[2048]{0:T(1024)S(1)}, f32[2048]{0:T(1024)}, u32[]{:S(2)}) copy-start(f32[2048]{0:T(1024)} %copy-done.14) | copy-start | bytes 24580
  56.1 5.1 %copy-start.21 = (bf16[256,256]{1,0:T(8,128)(2,1)S(1)}, bf16[256,256]{1,0:T(8,128)(2,1)}, u32[]{:S(2)}) copy-start(bf16[256,256]{1,0:T(8,128)(2,1)} %param.10) | copy-start | bytes 393220
  65.6 6.6 %slice-start = ((s8[6291456]{0:T(1024)(128)(4,1)}), s8[2097152]{0:T(1024)(128)(4,1)S(1)}, s32[]{:S(2)}) async-start(s8[6291456]{0:T(1024)(128)(4,1)} %bitcast.54), calls=%async_computation | async-start | bytes 4194304
  67.8 4.4 %slice-start.1 = ((s8[6291456]{0:T(1024)(128)(4,1)}), s8[4194304]{0:T(1024)(128)(4,1)S(1)}, s32[]{:S(2)}) async-start(s8[6291456]{0:T(1024)(128)(4,1)} %bitcast.54), calls=%async_computation.1 | async-start | bytes 8388608
  67.8 4.5 %copy-start.6 = (bf16[2048,128]{1,0:T(8,128)(2,1)S(1)}, bf16[2048,128]{1,0:T(8,128)(2,1)}, u32[]{:S(2)}) copy-start(bf16[2048,128]{1,0:T(8,128)(2,1)} %reshape.65) | copy-start | bytes 1572868
  67.8 4.5 %copy-start.11 = (bf16[512,256]{1,0:T(8,128)(2,1)S(1)}, bf16[512,256]{1,0:T(8,128)(2,1)}, u32[]{:S(2)}) copy-start(bf16[512,256]{1,0:T(8,128)(2,1)} %copy-done.8) | copy-start | bytes 786436
  67.8 4.5 %copy-start.13 = (f32[2048]{0:T(1024)S(1)}, f32[2048]{0:T(1024)}, u32[]{:S(2)}) copy-start(f32[2048]{0:T(1024)} %copy-done.12) | copy-start | bytes 24580
  67.8 4.5 %copy-start.22 = (bf16[256,256]{1,0:T(8,128)(2,1)S(1)}, bf16[256,256]{1,0:T(8,128)(2,1)}, u32[]{:S(2)}) copy-start(bf16[256,256]{1,0:T(8,128)(2,1)} %param.10) | copy-start | bytes 393220
  67.9 5.9 %slice-start.4 = ((s8[6291456]{0:T(1024)(128)(4,1)}), s8[4194304]{0:T(1024)(128)(4,1)S(1)}, s32[]{:S(2)}) async-start(s8[6291456]{0:T(1024)(128)(4,1)} %bitcast.58), calls=%async_computation.4 | async-start | bytes 8388608
  67.9 6.9 %slice-start.6 = ((s8[6291456]{0:T(1024)(128)(4,1)}), s8[4194304]{0:T(1024)(128)(4,1)S(1)}, s32[]{:S(2)}) async-start(s8[6291456]{0:T(1024)(128)(4,1)} %bitcast.60), calls=%async_computation.6 | async-start | bytes 8388608
  72.3 3.2 %slice-start.5 = ((s8[6291456]{0:T(1024)(128)(4,1)}), s8[2097152]{0:T(1024)(128)(4,1)S(1)}, s32[]{:S(2)}) async-start(s8[6291456]{0:T(1024)(128)(4,1)} %bitcast.58), calls=%async_computation.5 | async-start | bytes 4194304
  72.3 3.8 %slice-start.7 = ((s8[6291456]{0:T(1024)(128)(4,1)}), s8[2097152]{0:T(1024)(128)(4,1)S(1)}, s32[]{:S(2)}) async-start(s8[6291456]{0:T(1024)(128)(4,1)} %bitcast.60), calls=%async_computation.7 | async-start | bytes 4194304
  72.4 3.8 %copy-start.16 = (f32[2048]{0:T(1024)S(1)}, f32[2048]{0:T(1024)}, u32[]{:S(2)}) copy-start(f32[2048]{0:T(1024)} %copy-done.14) | copy-start | bytes 24580
  72.4 3.8 %copy-start.17 = (f32[2048]{0:T(1024)S(1)}, f32[2048]{0:T(1024)}, u32[]{:S(2)}) copy-start(f32[2048]{0:T(1024)} %get-tuple-element.44) | copy-start | bytes 24580
  79.1 5.0 %copy-start.3 = (bf16[768,128]{0,1:T(8,128)(2,1)}, bf16[768,128]{0,1:T(8,128)(2,1)S(1)}, u32[]{:S(2)}) copy-start(bf16[768,128]{0,1:T(8,128)(2,1)S(1)} %fusion.50) | copy-start | bytes 589828
  81.9 2.2 %copy-start.5 = (bf16[768,128]{0,1:T(8,128)(2,1)S(1)}, bf16[768,128]{0,1:T(8,128)(2,1)}, u32[]{:S(2)}) copy-start(bf16[768,128]{0,1:T(8,128)(2,1)} %fusion.9) | copy-start | bytes 589828
  85.0 21.9 %collective-permute-start.6 = (bf16[2,128,256]{1,2,0:T(8,128)(2,1)}, bf16[2,128,256]{1,2,0:T(8,128)(2,1)S(1)}, u32[]{:S(2)}, u32[]{:S(2)}) collective-permute-start(bf16[2,128,256]{1,2,0:T(8,128)(2,1)} %get-tuple-element.26), channel_id=1, source_target_pairs={{0,64},{1,65},{2,66},{3,67},{4,68},{5,69},{6,70},{7,71},{8,72},{9,... | collective-permute-start | bytes 393224 | tf_op jit(solution)/shard_map/ppermute | solution.py:15
  86.3 23.0 %collective-permute-start.7 = (bf16[2,128,256]{1,2,0:T(8,128)(2,1)}, bf16[2,128,256]{1,2,0:T(8,128)(2,1)S(1)}, u32[]{:S(2)}, u32[]{:S(2)}) collective-permute-start(bf16[2,128,256]{1,2,0:T(8,128)(2,1)} %get-tuple-element.27), channel_id=1, source_target_pairs={{64,0},{65,1},{66,2},{67,3},{68,4},{69,5},{70,6},{71,7},{72,8},{73... | collective-permute-start | bytes 393224 | tf_op jit(solution)/shard_map/ppermute | solution.py:15
  87.6 21.7 %collective-permute-start.8 = (bf16[2,128,256]{1,2,0:T(8,128)(2,1)S(1)}, bf16[2,128,256]{1,2,0:T(8,128)(2,1)S(1)}, u32[]{:S(2)}, u32[]{:S(2)}) collective-permute-start(bf16[2,128,256]{1,2,0:T(8,128)(2,1)S(1)} %get-tuple-element.28), channel_id=1, source_target_pairs={{0,128},{1,129},{2,130},{3,131},{4,132},{5,133},{6,134},{7,135},{8... | collective-permute-start | bytes 393224 | tf_op jit(solution)/shard_map/ppermute | solution.py:15
  94.9 14.5 %collective-permute-start.9 = (bf16[2,128,256]{1,2,0:T(8,128)(2,1)S(1)}, bf16[2,128,256]{1,2,0:T(8,128)(2,1)}, u32[]{:S(2)}, u32[]{:S(2)}) collective-permute-start(bf16[2,128,256]{1,2,0:T(8,128)(2,1)S(1)} %get-tuple-element.29), channel_id=1, source_target_pairs={{128,0},{129,1},{130,2},{131,3},{132,4},{133,5},{134,6},{135,7},{1... | collective-permute-start | bytes 393224 | tf_op jit(solution)/shard_map/ppermute | solution.py:15
  96.2 13.1 %collective-permute-start.10 = (bf16[2,128,256]{1,2,0:T(8,128)(2,1)S(1)}, bf16[2,128,256]{1,2,0:T(8,128)(2,1)}, u32[]{:S(2)}, u32[]{:S(2)}) collective-permute-start(bf16[2,128,256]{1,2,0:T(8,128)(2,1)S(1)} %get-tuple-element.30), channel_id=1, source_target_pairs={{0,192},{1,193},{2,194},{3,195},{4,196},{5,197},{6,198},{7,199},{8... | collective-permute-start | bytes 393224 | tf_op jit(solution)/shard_map/ppermute | solution.py:15
  107.0 8.1 %collective-permute-start.11 = (bf16[2,128,256]{1,2,0:T(8,128)(2,1)S(1)}, bf16[2,128,256]{1,2,0:T(8,128)(2,1)S(1)}, u32[]{:S(2)}, u32[]{:S(2)}) collective-permute-start(bf16[2,128,256]{1,2,0:T(8,128)(2,1)S(1)} %get-tuple-element.31), channel_id=1, source_target_pairs={{192,0},{193,1},{194,2},{195,3},{196,4},{197,5},{198,6},{199,7},{2... | collective-permute-start | bytes 393224 | tf_op jit(solution)/shard_map/ppermute | solution.py:15
where the time goes:
time: 118 us
  starting transfers between devices  34.6 us (29%)
  local copies, waits for them, and re-layouts  30.1 us (26%)
  matrix products  26.4 us (22%)
  other arithmetic  15.4 us (13%)
  waiting for transfers between devices  9.73 us (8%)
  between operations  1.35 us (1%)
    ppermute x12, starting transfers between devices, shifted(): return lax.ppermute(block, axis, route)  34.6 us
    unnamed x71, local copies, waits for them, and re-layouts  14.3 us
    ppermute x12, waiting for transfers between devices, shifted(): return lax.ppermute(block, axis, route)  9.73 us
    dot_general x2, matrix products, head_pass(): jnp.dot(weights_low.T, grad_rows, preferred_element_type=jnp.float32)  9.47 us
    dot_general x2, matrix products, head_pass(): jnp.dot(grad_rows, value_rows.T, preferred_element_type=jnp.float32)  5.77 us
    reshape x2, local copies, waits for them, and re-layouts, device_block(): grad_live[:, kv_head * width_cols:(kv_head + 1) * width_cols]  4.43 us
    dot_general x2, matrix products, head_pass(): jnp.dot(weights_low, value_rows, preferred_element_type=jnp.float32)  4.2 us
    convert_element_type x2, other arithmetic, head_pass(): (weights * (pressure - centre) * HEAD_DIM ** (-0.5)).astype(jnp.bfloat16)  3.49 us
  transfers between devices with their start and end apart: 12, of which 2 were waited for; matrix products, arithmetic and copies ran while one was open for 16% of the time, Pallas kernels for 0%

commit v1 on v0

v1 whole, which is shorter than its diff:
```python
import jax
import jax.numpy as jnp
from jax import lax
from jax.experimental import pallas as pl
from jax.experimental.pallas import tpu as pltpu
from jax.sharding import PartitionSpec as P

QUERY_HEADS = 16
KV_HEADS = 2
GROUP_HEADS = QUERY_HEADS // KV_HEADS
HEAD_DIM = 128
GROUP = 4
ROWS = 256
HALF = 128
SHARD = 128
REMOTE = (GROUP - 1) * SHARD
SCALE = HEAD_DIM**-0.5
EXP2_SCALE = SCALE * 1.4426950408889634
NEG = -1e30
F32 = jnp.float32
BF16 = jnp.bfloat16
VM = pltpu.VMEM


def dot_nt(a, b):
    return lax.dot_general(a, b, (((1,), (1,)), ((), ())), preferred_element_type=F32)


def dot_nn(a, b):
    return lax.dot_general(a, b, (((1,), (0,)), ((), ())), preferred_element_type=F32)


def col_max(x):
    return jnp.max(x, axis=0, keepdims=True)


def col_sum(x):
    return jnp.sum(x, axis=0, keepdims=True)


def second_half(a, b):
    return jnp.concatenate([a[HALF:], b[HALF:]], axis=0)


def halves(a, b):
    return jnp.concatenate([a[:, HALF:], b[:, HALF:]], axis=1)


def unhalves(x, which, fill):
    return jnp.concatenate([fill, x[:, which * HALF : (which + 1) * HALF]], axis=1)


def local_forward(
    q_in, do_in, pk, pv, rk, rv, slot_in, pos_in,
    q, do, kv, p1, dp1, p2, dp2, m_out, l_out, c_out, live,
    bias, slot, pos, sems,
):
    width = GROUP_HEADS * HEAD_DIM
    pieces = [
        (slot_in, slot),
        (pos_in, pos),
        (pk, kv.at[0, pl.ds(0, SHARD)]),
        (rk, kv.at[0, pl.ds(SHARD, ROWS)]),
        (pv, kv.at[1, pl.ds(0, SHARD)]),
        (rv, kv.at[1, pl.ds(SHARD, ROWS)]),
    ]
    for g in range(KV_HEADS):
        span = pl.ds(g * width, width)
        pieces.append((q_in.at[:, span], q.at[:, span]))
        pieces.append((do_in.at[:, span], do.at[:, span]))
    copies = [pltpu.make_async_copy(a, b, sems.at[n]) for n, (a, b) in enumerate(pieces)]
    for copy in copies:
        copy.start()
    copies[0].wait()
    copies[1].wait()
    slot_row = jnp.broadcast_to(slot[...], (ROWS, ROWS)).astype(F32)
    pos_row = jnp.broadcast_to(pos[...], (ROWS, ROWS)).astype(F32)
    slot_col = slot_row.T
    pos_col = pos_row.T
    seen = (slot_col == slot_row) & (slot_col >= 0) & (pos_col <= pos_row)
    bias[...] = jnp.where(seen, 0.0, NEG)
    live[...] = (slot[...] >= 0).astype(F32)
    nothing = jnp.full((1, HALF), NEG, F32)
    zero = jnp.zeros((1, HALF), F32)
    near = SHARD + HALF
    for copy in copies[2:6]:
        copy.wait()
    for g in range(KV_HEADS):
        copies[6 + 2 * g].wait()
        copies[7 + 2 * g].wait()
        cols = slice(g * HEAD_DIM, (g + 1) * HEAD_DIM)
        k1 = kv[0, :near, cols]
        v1 = kv[1, :near, cols]
        k2 = kv[0, near:, cols]
        v2 = kv[1, near:, cols]
        for pair in range(GROUP_HEADS // 2):
            first = g * GROUP_HEADS + 2 * pair
            qs = [q[:, h * HEAD_DIM : (h + 1) * HEAD_DIM] for h in (first, first + 1)]
            ds = [do[:, h * HEAD_DIM : (h + 1) * HEAD_DIM] for h in (first, first + 1)]
            b2 = bias[HALF:, HALF:]
            s2 = dot_nt(k2, second_half(*qs)) + jnp.concatenate([b2, b2], axis=1)
            m2 = col_max(s2)
            ms, ls, cs = [], [], []
            for i in range(2):
                s1 = dot_nt(k1, qs[i])
                s1 = jnp.concatenate([s1[:SHARD], s1[SHARD:] + bias[:HALF, :]], axis=0)
                m = jnp.maximum(col_max(s1), unhalves(m2, i, nothing))
                e1 = jnp.exp2((s1 - m) * EXP2_SCALE)
                g1 = dot_nt(v1, ds[i])
                p1[first + i] = e1
                dp1[first + i] = g1
                ms.append(m)
                ls.append(col_sum(e1))
                cs.append(col_sum(e1 * g1))
            e2 = jnp.exp2((s2 - halves(*ms)) * EXP2_SCALE)
            g2 = dot_nt(v2, second_half(*ds))
            p2[first // 2] = e2
            dp2[first // 2] = g2
            l2 = col_sum(e2)
            c2 = col_sum(e2 * g2)
            for i in range(2):
                h = first + i
                m_out[h : h + 1, :] = ms[i]
                l_out[h : h + 1, :] = ls[i] + unhalves(l2, i, zero)
                c_out[h : h + 1, :] = cs[i] + unhalves(c2, i, zero)


def remote_pass(
    q, do, r1, r2, r3, live, m_in, l_in, c_in, w_out, ds_out, f_out, d_out, g1, g2, g3
):
    shards = (r1, r2, r3)
    outs = (g1, g2, g3)
    alive = live[...]
    blocks = [slice(n * SHARD, (n + 1) * SHARD) for n in range(GROUP - 1)]
    columns = [slice(g * HEAD_DIM, (g + 1) * HEAD_DIM) for g in range(KV_HEADS)]
    keys = [jnp.concatenate([r[0, :, c] for r in shards], axis=0) for c in columns]
    values = [jnp.concatenate([r[1, :, c] for r in shards], axis=0) for c in columns]

    def head(ref, h):
        return ref[:, h * HEAD_DIM : (h + 1) * HEAD_DIM]

    def slopes_of(h):
        g = h // GROUP_HEADS
        s = dot_nt(keys[g], head(q, h))
        pressure = dot_nt(values[g], head(do, h))
        m_old = m_in[h : h + 1, :]
        tops = [col_max(s[b]) for b in blocks]
        es = [jnp.exp2((s[b] - top) * EXP2_SCALE) for b, top in zip(blocks, tops)]
        m = m_old
        for top in tops:
            m = jnp.maximum(m, top)
        back = jnp.exp2((m_old - m) * EXP2_SCALE)
        total = l_in[h : h + 1, :] * back
        centre = c_in[h : h + 1, :] * back
        factors = []
        for b, top, e in zip(blocks, tops, es):
            factor = jnp.exp2((top - m) * EXP2_SCALE)
            total = total + col_sum(e) * factor
            centre = centre + col_sum(e * pressure[b]) * factor
            factors.append(factor)
        inv = 1.0 / total
        centre = centre * inv
        inv = inv * alive
        f_out[h : h + 1, :] = back * inv
        d_out[h : h + 1, :] = centre
        lows, slopes = [], []
        for b, e, factor in zip(blocks, es, factors):
            w = e * (factor * inv)
            lows.append(w.astype(BF16))
            slopes.append((w * (pressure[b] - centre)).astype(BF16))
            w_out[h, b] = lows[-1]
            ds_out[h, b] = slopes[-1]
        return jnp.concatenate(lows, axis=0), jnp.concatenate(slopes, axis=0)

    made = {}
    dk = dv = None
    for t in range(QUERY_HEADS + GROUP_HEADS):
        if t < QUERY_HEADS:
            made[t] = slopes_of(t)
        h = t - GROUP_HEADS
        if h < 0:
            continue
        low, slopes = made.pop(h)
        k = dot_nn(slopes, head(q, h))
        v = dot_nn(low, head(do, h))
        first = h % GROUP_HEADS == 0
        dk = k if first else dk + k
        dv = v if first else dv + v
        if h % GROUP_HEADS == GROUP_HEADS - 1:
            cols = columns[h // GROUP_HEADS]
            for b, out in zip(blocks, outs):
                out[0, :, cols] = (dk[b] * SCALE).astype(BF16)
                out[1, :, cols] = dv[b].astype(BF16)


def local_backward(
    q, do, kv, r1, r2, r3, p1, dp1, p2, dp2, w_in, ds_in, f_in, d_in,
    out, dq, drk, drv, own,
):
    near = SHARD + HALF
    far = near + REMOTE
    for g in range(KV_HEADS):
        cols = slice(g * HEAD_DIM, (g + 1) * HEAD_DIM)
        shards = (r1, r2, r3)
        k_t = jnp.concatenate(
            [kv[0, :near, cols]] + [r[0, :, cols] for r in shards] + [kv[0, near:, cols]], axis=0
        ).T
        v_t = jnp.concatenate(
            [kv[1, :near, cols]] + [r[1, :, cols] for r in shards] + [kv[1, near:, cols]], axis=0
        ).T
        dk1 = jnp.zeros((near, HEAD_DIM), F32)
        dv1 = jnp.zeros((near, HEAD_DIM), F32)
        dk2 = jnp.zeros((HALF, HEAD_DIM), F32)
        dv2 = jnp.zeros((HALF, HEAD_DIM), F32)
        for pair in range(GROUP_HEADS // 2):
            first = g * GROUP_HEADS + 2 * pair
            qs = [q[:, h * HEAD_DIM : (h + 1) * HEAD_DIM] for h in (first, first + 1)]
            ds = [do[:, h * HEAD_DIM : (h + 1) * HEAD_DIM] for h in (first, first + 1)]
            fs = [f_in[h : h + 1, :] for h in (first, first + 1)]
            cs = [d_in[h : h + 1, :] for h in (first, first + 1)]
            w2 = p2[first // 2] * halves(*fs)
            s2 = (w2 * (dp2[first // 2] - halves(*cs))).astype(BF16)
            w2 = w2.astype(BF16)
            dk2 = dk2 + dot_nn(s2, second_half(*qs))
            dv2 = dv2 + dot_nn(w2, second_half(*ds))
            o2 = dot_nn(v_t[:, far:], w2)
            dq2 = dot_nn(k_t[:, far:], s2)
            for i in range(2):
                h = first + i
                w1 = p1[h] * fs[i]
                s1 = (w1 * (dp1[h] - cs[i])).astype(BF16)
                w1 = w1.astype(BF16)
                dk1 = dk1 + dot_nn(s1, qs[i])
                dv1 = dv1 + dot_nn(w1, ds[i])
                half = slice(i * HALF, (i + 1) * HALF)
                o = dot_nn(v_t[:, :near], w1) + dot_nn(v_t[:, near:far], w_in[h])
                gq = dot_nn(k_t[:, :near], s1) + dot_nn(k_t[:, near:far], ds_in[h])
                o = jnp.concatenate([o[:, :HALF], o[:, HALF:] + o2[:, half]], axis=1)
                gq = jnp.concatenate([gq[:, :HALF], gq[:, HALF:] + dq2[:, half]], axis=1)
                out[:, h * HEAD_DIM : (h + 1) * HEAD_DIM] = o.T.astype(BF16)
                dq[:, h * HEAD_DIM : (h + 1) * HEAD_DIM] = (gq.T * SCALE).astype(BF16)
        dk1 = dk1 * SCALE
        own[0, :, cols] = dk1[:SHARD].astype(BF16)
        own[1, :, cols] = dv1[:SHARD].astype(BF16)
        drk[:HALF, cols] = dk1[SHARD:].astype(BF16)
        drv[:HALF, cols] = dv1[SHARD:].astype(BF16)
        drk[HALF:, cols] = (dk2 * SCALE).astype(BF16)
        drv[HALF:, cols] = dv2.astype(BF16)


def add_partials(a, b, c, d, keys, values):
    keys[...] = (
        (a[0].astype(F32) + b[0].astype(F32)) + (c[0].astype(F32) + d[0].astype(F32))
    ).astype(BF16)
    values[...] = (
        (a[1].astype(F32) + b[1].astype(F32)) + (c[1].astype(F32) + d[1].astype(F32))
    ).astype(BF16)


def in_vmem(x):
    return pltpu.with_memory_space_constraint(x, pltpu.VMEM)


def in_hbm(x):
    return pltpu.with_memory_space_constraint(x, pltpu.HBM)


def call(body, name, ins, outs, scratch=(), in_space=pltpu.VMEM, flops=0):
    return pl.pallas_call(
        body,
        name=name,
        in_specs=[pl.BlockSpec(memory_space=in_space)] * len(ins),
        out_specs=[pl.BlockSpec(memory_space=pltpu.VMEM)] * len(outs),
        out_shape=outs,
        scratch_shapes=list(scratch),
        cost_estimate=pl.CostEstimate(flops=flops, bytes_accessed=1 << 20, transcendentals=0),
        compiler_params=pltpu.CompilerParams(vmem_limit_bytes=24 * 1024 * 1024),
    )(*ins)


def per_device(
    query, response_keys, response_values, prompt_keys, prompt_values, dout, row_slot, row_pos
):
    devices = lax.axis_size("rows")
    stride = devices // GROUP
    hbm = jax.ShapeDtypeStruct
    width = KV_HEADS * HEAD_DIM
    heads = (QUERY_HEADS, ROWS)
    stacked = jnp.stack([prompt_keys, prompt_values])

    def moved(block, steps):
        route = [(i, (i + steps * stride) % devices) for i in range(devices)]
        return lax.ppermute(block, "rows", route)

    remote = [moved(stacked, steps) for steps in (1, 3, 2)]
    slot = row_slot.reshape(1, ROWS)
    pos = row_pos.reshape(1, ROWS)
    pair_heads = QUERY_HEADS // 2
    near = SHARD + HALF
    arrays = (
        query, dout, prompt_keys, prompt_values, response_keys, response_values, slot, pos
    )
    q, do, kv, p1, dp1, p2, dp2, m, l, c, live = map(
        in_vmem,
        call(
            local_forward,
            "local_forward",
            [in_hbm(x) for x in arrays],
            [
                VM(query.shape, BF16),
                VM(query.shape, BF16),
                VM((2, SHARD + ROWS, width), BF16),
                VM((QUERY_HEADS, near, ROWS), F32),
                VM((QUERY_HEADS, near, ROWS), F32),
                VM((pair_heads, HALF, ROWS), F32),
                VM((pair_heads, HALF, ROWS), F32),
                VM(heads, F32),
                VM(heads, F32),
                VM(heads, F32),
                VM((1, ROWS), F32),
            ],
            [
                VM((ROWS, ROWS), F32),
                VM((1, ROWS), jnp.int32),
                VM((1, ROWS), jnp.int32),
                pltpu.SemaphoreType.DMA((6 + 2 * KV_HEADS,)),
            ],
            in_space=pltpu.HBM,
            flops=10**9,
        ),
    )
    partial = (2, SHARD, width)
    w, ds, f, d, g1, g2, g3 = call(
        remote_pass,
        "remote_pass",
        [q, do, *remote, live, m, l, c],
        [
            VM((QUERY_HEADS, REMOTE, ROWS), BF16),
            VM((QUERY_HEADS, REMOTE, ROWS), BF16),
            VM(heads, F32),
            VM(heads, F32),
            hbm(partial, BF16),
            hbm(partial, BF16),
            hbm(partial, BF16),
        ],
        flops=2 * 10**9,
    )
    back = [moved(g, -steps) for g, steps in ((g1, 1), (g2, 3), (g3, 2))]
    out, dq, drk, drv, own = call(
        local_backward,
        "local_backward",
        [q, do, kv, *remote, p1, dp1, p2, dp2] + [in_vmem(x) for x in (w, ds, f, d)],
        [
            hbm(query.shape, BF16),
            hbm(query.shape, BF16),
            hbm(response_keys.shape, BF16),
            hbm(response_keys.shape, BF16),
            hbm(partial, BF16),
        ],
        flops=3 * 10**9,
    )
    gpk, gpv = call(
        add_partials,
        "add_partials",
        [own, *back],
        [hbm(prompt_keys.shape, BF16), hbm(prompt_keys.shape, BF16)],
    )
    return out, dq, drk, drv, gpk, gpv


def solution(mesh):
    rows = P("rows", None)
    return jax.shard_map(
        per_device,
        mesh=mesh,
        in_specs=(rows,) * 6 + (P("rows"),) * 2,
        out_specs=(rows,) * 6,
        check_vma=False,
    )
```

time: 118 us -> 29.2 us (0.25)
  local copies, waits for them, and re-layouts: 30.1 us -> 0 us
  matrix products: 26.4 us -> 0 us
  starting transfers between devices: 34.6 us -> 9.73 us
  other arithmetic: 15.4 us -> 0.89 us
  Pallas kernels: 0 us -> 14.5 us
  waiting for transfers between devices: 9.73 us -> 3.03 us
    dot_general x12 -> x0, matrix products: 26.4 us -> none  [the longest x2 9.47 us: head_pass(): jnp.dot(weights_low.T, grad_rows, preferred_element_type=jnp.float32)]
    ppermute x12 -> x6, starting transfers between devices: 34.6 us -> 9.73 us  [moved(): return lax.ppermute(block, 'rows', route)]
    pallas_call x0 -> x4, Pallas kernels: none -> 14.5 us  [call(): pl.pallas_call(body, name=name, in_specs=[pl.BlockSpec(memory_space=in_sp...]
    unnamed x71 -> x0, local copies, waits for them, and re-layouts: 14.3 us -> none
    reshape x8 -> x0, local copies, waits for them, and re-layouts: 9.95 us -> none  [the longest x2 4.43 us: device_block(): grad_live[:, kv_head * width_cols:(kv_head + 1) * width_cols]]
    ppermute x12 -> x6, waiting for transfers between devices: 9.73 us -> 3.03 us  [moved(): return lax.ppermute(block, 'rows', route)]
    convert_element_type x2 -> x0, other arithmetic: 3.49 us -> none  [head_pass(): (weights * (pressure - centre) * HEAD_DIM ** (-0.5)).astype(jnp.bfloat16)]
    slice x2 -> x0, local copies, waits for them, and re-layouts: 3.31 us -> none  [the longest x1 2.27 us: device_block(): query[:, kv_head * width_cols:(kv_head + 1) * width_cols]]
  transfers between devices with their start and end apart: 12 -> 6, of which waited for: 2 -> 3; matrix products, arithmetic and copies ran while one was open for 16% -> 0% of each run, Pallas kernels for 0% -> 31%
where the time goes in v1:
time: 29.2 us; the launch traced here: 28.8 us
  Pallas kernels  14.5 us (50%)
  starting transfers between devices  9.73 us (33%)
  waiting for transfers between devices  3.03 us (10%)
  other arithmetic  0.89 us (3%)
  between operations  0.66 us (2%)
    pallas_call x4, Pallas kernels, call(): pl.pallas_call(body, name=name, in_specs=[pl.BlockSpec(memory_space=in_sp...  14.5 us
    ppermute x6, starting transfers between devices, moved(): return lax.ppermute(block, 'rows', route)  9.73 us
    ppermute x6, waiting for transfers between devices, moved(): return lax.ppermute(block, 'rows', route)  3.03 us
    another operation x1, other arithmetic, per_device(): stacked = jnp.stack([prompt_keys, prompt_values])  0.89 us
  transfers between devices with their start and end apart: 6, of which 3 were waited for; matrix products, arithmetic and copies ran while one was open for 0% of the time, Pallas kernels for 31%

profile of v1, /device:TPU:96, one launch (start us, length us, event | category | flops | bytes accessed | tf_op | source)
XLA Modules:
  0.0 28.8 jit_solution(139376472657308064)
XLA Ops:
  0.6 0.9 %pad_maximum_fusion = bf16[2,128,256]{2,1,0:T(8,128)(2,1)S(1)} fusion(bf16[1,128,256]{2,1,0:T(8,128)(2,1)} %bitcast.5, bf16[1,128,256]{2,1,0:T(8,128)(2,1)} %bitcast.4), kind=kLoop, calls=%fused_computation | loop fusion | flops 65536 | bytes 262144 | tf_op jit(solution)/shard_map/stack | solution.py:289
  1.5 3.3 %collective-permute-start.2 = (bf16[2,128,256]{2,1,0:T(8,128)(2,1)S(1)}, bf16[2,128,256]{2,1,0:T(8,128)(2,1)S(1)}, u32[]{:S(2)}, u32[]{:S(2)}) collective-permute-start(bf16[2,128,256]{2,1,0:T(8,128)(2,1)S(1)} %pad_maximum_fusion), channel_id=1, source_target_pairs={{0,128},{1,129},{2,130},{3,131},{4,132},{5,133},{6,134},{7,135},{8... | collective-permute-start | bytes 393224 | tf_op jit(solution)/shard_map/ppermute | solution.py:293
  4.8 1.1 %collective-permute-start.1 = (bf16[2,128,256]{2,1,0:T(8,128)(2,1)S(1)}, bf16[2,128,256]{2,1,0:T(8,128)(2,1)S(1)}, u32[]{:S(2)}, u32[]{:S(2)}) collective-permute-start(bf16[2,128,256]{2,1,0:T(8,128)(2,1)S(1)} %pad_maximum_fusion), channel_id=1, source_target_pairs={{0,192},{1,193},{2,194},{3,195},{4,196},{5,197},{6,198},{7,199},{8... | collective-permute-start | bytes 393224 | tf_op jit(solution)/shard_map/ppermute | solution.py:293
  5.9 1.0 %collective-permute-start = (bf16[2,128,256]{2,1,0:T(8,128)(2,1)S(1)}, bf16[2,128,256]{2,1,0:T(8,128)(2,1)S(1)}, u32[]{:S(2)}, u32[]{:S(2)}) collective-permute-start(bf16[2,128,256]{2,1,0:T(8,128)(2,1)S(1)} %pad_maximum_fusion), channel_id=1, source_target_pairs={{0,64},{1,65},{2,66},{3,67},{4,68},{5,69},{6,70},{7,71},{8,72},{9,... | collective-permute-start | bytes 393224 | tf_op jit(solution)/shard_map/ppermute | solution.py:293
  6.8 3.8 %local_forward.1 = (bf16[256,2048]{1,0:T(8,128)(2,1)S(1)}, bf16[256,2048]{1,0:T(8,128)(2,1)S(1)}, bf16[2,384,256]{2,1,0:T(8,128)(2,1)S(1)}, f32[16,256,256]{2,1,...) custom-call(bf16[256,2048]{1,0:T(8,128)(2,1)} %q_in.1, ...), custom_call_target="tpu_custom_call" | custom-call | flops 1000000000 | bytes 1048576 | tf_op jit(solution)/shard_map/local_forward/pallas_call | solution.py:269
  10.6 0.0 collective-permute-done.2.r3
  10.7 0.8 %collective-permute-done.1.r2 = bf16[2,128,256]{2,1,0:T(8,128)(2,1)S(1)} collective-permute-done((bf16[2,128,256]{2,1,0:T(8,128)(2,1)S(1)}, bf16[2,128,256]{2,1,0:T(8,128)(2,1)S(1)}, u32[]{:S(2)}, u32[]{:S(2)}) %collective-permute-start.1) | collective-permute-done | bytes 131104 | tf_op jit(solution)/shard_map/ppermute | solution.py:293
  11.5 0.5 %collective-permute-done.r1 = bf16[2,128,256]{2,1,0:T(8,128)(2,1)S(1)} collective-permute-done((bf16[2,128,256]{2,1,0:T(8,128)(2,1)S(1)}, bf16[2,128,256]{2,1,0:T(8,128)(2,1)S(1)}, u32[]{:S(2)}, u32[]{:S(2)}) %collective-permute-start) | collective-permute-done | bytes 131104 | tf_op jit(solution)/shard_map/ppermute | solution.py:293
  12.0 4.8 %remote_pass.1 = (bf16[16,384,256]{2,1,0:T(8,128)(2,1)S(1)}, bf16[16,384,256]{2,1,0:T(8,128)(2,1)S(1)}, f32[16,256]{1,0:T(8,128)S(1)}, f32[16,256]{1,0:T(8,128)S...) custom-call(bf16[256,2048]{1,0:T(8,128)(2,1)S(1)} %get-tuple-element.31.q,, ...), custom_call_target="tpu_custom_call" | custom-call | flops 2000000000 | bytes 1048576 | tf_op jit(solution)/shard_map/remote_pass/pallas_call | solution.py:269
  16.8 2.2 %collective-permute-start.3 = (bf16[2,128,256]{2,1,0:T(8,128)(2,1)S(1)}, bf16[2,128,256]{2,1,0:T(8,128)(2,1)S(1)}, u32[]{:S(2)}, u32[]{:S(2)}) collective-permute-start(bf16[2,128,256]{2,1,0:T(8,128)(2,1)S(1)} %get-tuple-element.51), channel_id=1, source_target_pairs={{0,192},{1,193},{2,194},{3,195},{4,196},{5,197},{6,198},{7,199},{8... | collective-permute-start | bytes 393224 | tf_op jit(solution)/shard_map/ppermute | solution.py:293
  19.1 0.0 collective-permute-start.4
  19.1 2.2 %collective-permute-start.5 = (bf16[2,128,256]{2,1,0:T(8,128)(2,1)S(1)}, bf16[2,128,256]{2,1,0:T(8,128)(2,1)S(1)}, u32[]{:S(2)}, u32[]{:S(2)}) collective-permute-start(bf16[2,128,256]{2,1,0:T(8,128)(2,1)S(1)} %get-tuple-element.53), channel_id=1, source_target_pairs={{0,128},{1,129},{2,130},{3,131},{4,132},{5,133},{6,134},{7,135},{8... | collective-permute-start | bytes 393224 | tf_op jit(solution)/shard_map/ppermute | solution.py:293
  21.3 5.2 %local_backward.1 = (bf16[256,2048]{1,0:T(8,128)(2,1)}, bf16[256,2048]{1,0:T(8,128)(2,1)}, bf16[256,256]{1,0:T(8,128)(2,1)}, bf16[256,256]{1,0:T(8,128)(2,1)}, bf16[2,128,256]{2,1,0:T(8,128)(2,1)S(1)}) custom-call(bf16[256,2048]{1,0:T(8,128)(2,1)S(1)} %get-tuple-element.31.q, bf16[256,2048]{1,0:T(8,128)(2,1)S(1)} %get-tuple-element.32.do, ...), custom_call_target="tpu_custom_call" | custom-call | flops 3000000000 | bytes 1048576 | tf_op jit(solution)/shard_map/local_backward/pallas_call | solution.py:269
  26.5 0.0 collective-permute-done.3.b
  26.5 1.6 %collective-permute-done.4.c = bf16[2,128,256]{2,1,0:T(8,128)(2,1)S(1)} collective-permute-done((bf16[2,128,256]{2,1,0:T(8,128)(2,1)S(1)}, bf16[2,128,256]{2,1,0:T(8,128)(2,1)S(1)}, u32[]{:S(2)}, u32[]{:S(2)}) %collective-permute-start.4) | collective-permute-done | bytes 131104 | tf_op jit(solution)/shard_map/ppermute | solution.py:293
  28.1 0.0 collective-permute-done.5.d
  28.1 0.7 %add_partials.1 = (bf16[128,256]{1,0:T(8,128)(2,1)}, bf16[128,256]{1,0:T(8,128)(2,1)}) custom-call(bf16[2,128,256]{2,1,0:T(8,128)(2,1)S(1)} %get-tuple-element.50.a, bf16[2,128,256]{2,1,0:T(8,128)(2,1)S(1)} %collective-permute-done.3.b, bf16[2,128,256]{2,1,0:T(8,128)(2,1)S(1)} %collective-permute-done.4.c, bf16[2,128,256]{2,1,0:T(8,128)(2,1)S(1)} %collective-permute-done.5.d), custom_call_target="tpu_custom_call" | custom-call | bytes 1048576 | tf_op jit(solution)/shard_map/add_partials/pallas_call | solution.py:269
Async XLA Ops:
  1.5 9.1 %collective-permute-start.2 = (bf16[2,128,256]{2,1,0:T(8,128)(2,1)S(1)}, bf16[2,128,256]{2,1,0:T(8,128)(2,1)S(1)}, u32[]{:S(2)}, u32[]{:S(2)}) collective-permute-start(bf16[2,128,256]{2,1,0:T(8,128)(2,1)S(1)} %pad_maximum_fusion), channel_id=1, source_target_pairs={{0,128},{1,129},{2,130},{3,131},{4,132},{5,133},{6,134},{7,135},{8... | collective-permute-start | bytes 393224 | tf_op jit(solution)/shard_map/ppermute | solution.py:293
  4.8 6.7 %collective-permute-start.1 = (bf16[2,128,256]{2,1,0:T(8,128)(2,1)S(1)}, bf16[2,128,256]{2,1,0:T(8,128)(2,1)S(1)}, u32[]{:S(2)}, u32[]{:S(2)}) collective-permute-start(bf16[2,128,256]{2,1,0:T(8,128)(2,1)S(1)} %pad_maximum_fusion), channel_id=1, source_target_pairs={{0,192},{1,193},{2,194},{3,195},{4,196},{5,197},{6,198},{7,199},{8... | collective-permute-start | bytes 393224 | tf_op jit(solution)/shard_map/ppermute | solution.py:293
  5.9 6.2 %collective-permute-start = (bf16[2,128,256]{2,1,0:T(8,128)(2,1)S(1)}, bf16[2,128,256]{2,1,0:T(8,128)(2,1)S(1)}, u32[]{:S(2)}, u32[]{:S(2)}) collective-permute-start(bf16[2,128,256]{2,1,0:T(8,128)(2,1)S(1)} %pad_maximum_fusion), channel_id=1, source_target_pairs={{0,64},{1,65},{2,66},{3,67},{4,68},{5,69},{6,70},{7,71},{8,72},{9,... | collective-permute-start | bytes 393224 | tf_op jit(solution)/shard_map/ppermute | solution.py:293
  16.8 9.6 %collective-permute-start.3 = (bf16[2,128,256]{2,1,0:T(8,128)(2,1)S(1)}, bf16[2,128,256]{2,1,0:T(8,128)(2,1)S(1)}, u32[]{:S(2)}, u32[]{:S(2)}) collective-permute-start(bf16[2,128,256]{2,1,0:T(8,128)(2,1)S(1)} %get-tuple-element.51), channel_id=1, source_target_pairs={{0,192},{1,193},{2,194},{3,195},{4,196},{5,197},{6,198},{7,199},{8... | collective-permute-start | bytes 393224 | tf_op jit(solution)/shard_map/ppermute | solution.py:293
  19.1 9.1 %collective-permute-start.4 = (bf16[2,128,256]{2,1,0:T(8,128)(2,1)S(1)}, bf16[2,128,256]{2,1,0:T(8,128)(2,1)S(1)}, u32[]{:S(2)}, u32[]{:S(2)}) collective-permute-start(bf16[2,128,256]{2,1,0:T(8,128)(2,1)S(1)} %get-tuple-element.52), channel_id=1, source_target_pairs={{0,64},{1,65},{2,66},{3,67},{4,68},{5,69},{6,70},{7,71},{8,72},{9,... | collective-permute-start | bytes 393224 | tf_op jit(solution)/shard_map/ppermute | solution.py:293
  19.1 9.1 %collective-permute-start.5 = (bf16[2,128,256]{2,1,0:T(8,128)(2,1)S(1)}, bf16[2,128,256]{2,1,0:T(8,128)(2,1)S(1)}, u32[]{:S(2)}, u32[]{:S(2)}) collective-permute-start(bf16[2,128,256]{2,1,0:T(8,128)(2,1)S(1)} %get-tuple-element.53), channel_id=1, source_target_pairs={{0,128},{1,129},{2,130},{3,131},{4,132},{5,133},{6,134},{7,135},{8... | collective-permute-start | bytes 393224 | tf_op jit(solution)/shard_map/ppermute | solution.py:293

commit v2 on v1

--- a/solution.py
+++ b/solution.py
@@ -10,6 +10,8 @@
 GROUP_HEADS = QUERY_HEADS // KV_HEADS
 HEAD_DIM = 128
 GROUP = 4
+STEPS = (3, 1, 2)
+SEND_ORDER = (0, 1, 2)
 ROWS = 256
 HALF = 128
 SHARD = 128
@@ -17,6 +19,8 @@
 SCALE = HEAD_DIM**-0.5
 EXP2_SCALE = SCALE * 1.4426950408889634
 NEG = -1e30
+LOAD_AT = (0, 4)
+LATE_SKEW = 2
 F32 = jnp.float32
 BF16 = jnp.bfloat16
 VM = pltpu.VMEM
@@ -55,7 +59,6 @@
     q, do, kv, p1, dp1, p2, dp2, m_out, l_out, c_out, live,
     bias, slot, pos, sems,
 ):
-    width = GROUP_HEADS * HEAD_DIM
     pieces = [
         (slot_in, slot),
         (pos_in, pos),
@@ -64,8 +67,8 @@
         (pv, kv.at[1, pl.ds(0, SHARD)]),
         (rv, kv.at[1, pl.ds(SHARD, ROWS)]),
     ]
-    for g in range(KV_HEADS):
-        span = pl.ds(g * width, width)
+    for n in range(QUERY_HEADS // 2):
+        span = pl.ds(n * 2 * HEAD_DIM, 2 * HEAD_DIM)
         pieces.append((q_in.at[:, span], q.at[:, span]))
         pieces.append((do_in.at[:, span], do.at[:, span]))
     copies = [pltpu.make_async_copy(a, b, sems.at[n]) for n, (a, b) in enumerate(pieces)]
@@ -86,8 +89,6 @@
     for copy in copies[2:6]:
         copy.wait()
     for g in range(KV_HEADS):
-        copies[6 + 2 * g].wait()
-        copies[7 + 2 * g].wait()
         cols = slice(g * HEAD_DIM, (g + 1) * HEAD_DIM)
         k1 = kv[0, :near, cols]
         v1 = kv[1, :near, cols]
@@ -95,6 +96,10 @@
         v2 = kv[1, near:, cols]
         for pair in range(GROUP_HEADS // 2):
             first = g * GROUP_HEADS + 2 * pair
+            if first in LOAD_AT:
+                stop = min([n for n in LOAD_AT if n > first] + [QUERY_HEADS])
+                for copy in copies[6 + first : 6 + stop]:
+                    copy.wait()
             qs = [q[:, h * HEAD_DIM : (h + 1) * HEAD_DIM] for h in (first, first + 1)]
             ds = [do[:, h * HEAD_DIM : (h + 1) * HEAD_DIM] for h in (first, first + 1)]
             b2 = bias[HALF:, HALF:]
@@ -125,59 +130,106 @@
                 c_out[h : h + 1, :] = cs[i] + unhalves(c2, i, zero)
 
 
-def remote_pass(
-    q, do, r1, r2, r3, live, m_in, l_in, c_in, w_out, ds_out, f_out, d_out, g1, g2, g3
-):
-    shards = (r1, r2, r3)
-    outs = (g1, g2, g3)
-    alive = live[...]
-    blocks = [slice(n * SHARD, (n + 1) * SHARD) for n in range(GROUP - 1)]
-    columns = [slice(g * HEAD_DIM, (g + 1) * HEAD_DIM) for g in range(KV_HEADS)]
-    keys = [jnp.concatenate([r[0, :, c] for r in shards], axis=0) for c in columns]
-    values = [jnp.concatenate([r[1, :, c] for r in shards], axis=0) for c in columns]
-
-    def head(ref, h):
-        return ref[:, h * HEAD_DIM : (h + 1) * HEAD_DIM]
-
-    def slopes_of(h):
-        g = h // GROUP_HEADS
-        s = dot_nt(keys[g], head(q, h))
-        pressure = dot_nt(values[g], head(do, h))
-        m_old = m_in[h : h + 1, :]
-        tops = [col_max(s[b]) for b in blocks]
-        es = [jnp.exp2((s[b] - top) * EXP2_SCALE) for b, top in zip(blocks, tops)]
+def head(ref, h):
+    return ref[:, h * HEAD_DIM : (h + 1) * HEAD_DIM]
+
+
+def columns_of(h):
+    g = h // GROUP_HEADS
+    return slice(g * HEAD_DIM, (g + 1) * HEAD_DIM)
+
+
+def block(n):
+    return slice(n * SHARD, (n + 1) * SHARD)
+
+
+def early_forward(q, do, rx, ry, m_in, l_in, c_in, e_out, p_out, tx, ty, m_out, l_out, c_out):
+    for h in range(QUERY_HEADS):
+        cols = columns_of(h)
+        row = slice(h, h + 1)
+        s = dot_nt(jnp.concatenate([rx[0, :, cols], ry[0, :, cols]], axis=0), head(q, h))
+        pressure = dot_nt(jnp.concatenate([rx[1, :, cols], ry[1, :, cols]], axis=0), head(do, h))
+        m_old = m_in[row, :]
         m = m_old
-        for top in tops:
+        tops, sums, centres = [], [], []
+        for n in range(2):
+            top = col_max(s[block(n)])
+            e = jnp.exp2((s[block(n)] - top) * EXP2_SCALE)
+            p = pressure[block(n)]
+            e_out[h, block(n)] = e
+            p_out[h, block(n)] = p
+            tops.append(top)
+            sums.append(col_sum(e))
+            centres.append(col_sum(e * p))
             m = jnp.maximum(m, top)
         back = jnp.exp2((m_old - m) * EXP2_SCALE)
-        total = l_in[h : h + 1, :] * back
-        centre = c_in[h : h + 1, :] * back
-        factors = []
-        for b, top, e in zip(blocks, tops, es):
+        total = l_in[row, :] * back
+        centre = c_in[row, :] * back
+        for top, a, b in zip(tops, sums, centres):
             factor = jnp.exp2((top - m) * EXP2_SCALE)
-            total = total + col_sum(e) * factor
-            centre = centre + col_sum(e * pressure[b]) * factor
-            factors.append(factor)
+            total = total + a * factor
+            centre = centre + b * factor
+        tx[row, :] = tops[0]
+        ty[row, :] = tops[1]
+        m_out[row, :] = m
+        l_out[row, :] = total
+        c_out[row, :] = centre
+
+
+def late_pass(
+    q, do, rz, live, m_first, tx, ty, m_in, l_in, c_in, e_in, p_in,
+    w_out, ds_out, f_out, d_out, gx, gy, gz,
+):
+    alive = live[...]
+
+    def slopes_of(h):
+        cols = columns_of(h)
+        row = slice(h, h + 1)
+        s = dot_nt(rz[0, :, cols], head(q, h))
+        pressure = dot_nt(rz[1, :, cols], head(do, h))
+        m_old = m_in[row, :]
+        top = col_max(s)
+        e = jnp.exp2((s - top) * EXP2_SCALE)
+        m = jnp.maximum(m_old, top)
+        back = jnp.exp2((m_old - m) * EXP2_SCALE)
+        factor = jnp.exp2((top - m) * EXP2_SCALE)
+        total = l_in[row, :] * back + col_sum(e) * factor
         inv = 1.0 / total
-        centre = centre * inv
+        centre = (c_in[row, :] * back + col_sum(e * pressure) * factor) * inv
         inv = inv * alive
-        f_out[h : h + 1, :] = back * inv
-        d_out[h : h + 1, :] = centre
+        f_out[row, :] = jnp.exp2((m_first[row, :] - m) * EXP2_SCALE) * inv
+        d_out[row, :] = centre
         lows, slopes = [], []
-        for b, e, factor in zip(blocks, es, factors):
-            w = e * (factor * inv)
+        for n, (a, b) in enumerate(
+            ((e_in[h, block(0)], p_in[h, block(0)]), (e_in[h, block(1)], p_in[h, block(1)]), (e, pressure))
+        ):
+            if n < 2:
+                factor = jnp.exp2(((tx, ty)[n][row, :] - m) * EXP2_SCALE)
+            else:
+                factor = jnp.exp2((top - m) * EXP2_SCALE)
+            w = a * (factor * inv)
             lows.append(w.astype(BF16))
-            slopes.append((w * (pressure[b] - centre)).astype(BF16))
-            w_out[h, b] = lows[-1]
-            ds_out[h, b] = slopes[-1]
+            slopes.append((w * (b - centre)).astype(BF16))
+            for half in range(2):
+                w_out[h, half, block(n)] = lows[-1][:, half * HALF : (half + 1) * HALF]
+                ds_out[h, half, block(n)] = slopes[-1][:, half * HALF : (half + 1) * HALF]
         return jnp.concatenate(lows, axis=0), jnp.concatenate(slopes, axis=0)
 
+    def store(cols, dk, dv):
+        for n, out in enumerate((gx, gy, gz)):
+            out[0, :, cols] = (dk[block(n)] * SCALE).astype(BF16)
+            out[1, :, cols] = dv[block(n)].astype(BF16)
+
+    skewed_terms(q, do, slopes_of, store, LATE_SKEW)
+
+
+def skewed_terms(q, do, slopes_of, store, skew):
     made = {}
     dk = dv = None
-    for t in range(QUERY_HEADS + GROUP_HEADS):
+    for t in range(QUERY_HEADS + skew):
         if t < QUERY_HEADS:
             made[t] = slopes_of(t)
-        h = t - GROUP_HEADS
+        h = t - skew
         if h < 0:
             continue
         low, slopes = made.pop(h)
@@ -187,21 +239,26 @@
         dk = k if first else dk + k
         dv = v if first else dv + v
         if h % GROUP_HEADS == GROUP_HEADS - 1:
-            cols = columns[h // GROUP_HEADS]
-            for b, out in zip(blocks, outs):
-                out[0, :, cols] = (dk[b] * SCALE).astype(BF16)
-                out[1, :, cols] = dv[b].astype(BF16)
+            store(columns_of(h), dk, dv)
 
 
 def local_backward(
-    q, do, kv, r1, r2, r3, p1, dp1, p2, dp2, w_in, ds_in, f_in, d_in,
-    out, dq, drk, drv, own,
+    q, do, kv, rx, ry, rz, p1, dp1, p2, dp2, w_in, ds_in, f_in, d_in,
+    out_hbm, dq_hbm, drk_hbm, drv_hbm, own,
+    out, dq, drk, drv, sems,
 ):
+    started = []
+
+    def send(buffer, target, cols):
+        copy = pltpu.make_async_copy(buffer.at[:, cols], target.at[:, cols], sems.at[len(started)])
+        copy.start()
+        started.append(copy)
+
     near = SHARD + HALF
-    far = near + REMOTE
+    unseen = jnp.zeros((HALF, HALF), BF16)
     for g in range(KV_HEADS):
         cols = slice(g * HEAD_DIM, (g + 1) * HEAD_DIM)
-        shards = (r1, r2, r3)
+        shards = (rx, ry, rz)
         k_t = jnp.concatenate(
             [kv[0, :near, cols]] + [r[0, :, cols] for r in shards] + [kv[0, near:, cols]], axis=0
         ).T
@@ -223,8 +280,6 @@
             w2 = w2.astype(BF16)
             dk2 = dk2 + dot_nn(s2, second_half(*qs))
             dv2 = dv2 + dot_nn(w2, second_half(*ds))
-            o2 = dot_nn(v_t[:, far:], w2)
-            dq2 = dot_nn(k_t[:, far:], s2)
             for i in range(2):
                 h = first + i
                 w1 = p1[h] * fs[i]
@@ -233,12 +288,12 @@
                 dk1 = dk1 + dot_nn(s1, qs[i])
                 dv1 = dv1 + dot_nn(w1, ds[i])
                 half = slice(i * HALF, (i + 1) * HALF)
-                o = dot_nn(v_t[:, :near], w1) + dot_nn(v_t[:, near:far], w_in[h])
-                gq = dot_nn(k_t[:, :near], s1) + dot_nn(k_t[:, near:far], ds_in[h])
-                o = jnp.concatenate([o[:, :HALF], o[:, HALF:] + o2[:, half]], axis=1)
-                gq = jnp.concatenate([gq[:, :HALF], gq[:, HALF:] + dq2[:, half]], axis=1)
-                out[:, h * HEAD_DIM : (h + 1) * HEAD_DIM] = o.T.astype(BF16)
-                dq[:, h * HEAD_DIM : (h + 1) * HEAD_DIM] = (gq.T * SCALE).astype(BF16)
+                ws = [w1, jnp.concatenate([w_in[h, 0], w_in[h, 1]], axis=1), jnp.concatenate([unseen, w2[:, half]], axis=1)]
+                ss = [s1, jnp.concatenate([ds_in[h, 0], ds_in[h, 1]], axis=1), jnp.concatenate([unseen, s2[:, half]], axis=1)]
+                o = dot_nn(v_t, jnp.concatenate(ws, axis=0))
+                gq = dot_nn(k_t, jnp.concatenate(ss, axis=0))
+                out[:, h * HEAD_DIM : (h + 1) * HEAD_DIM] = o.astype(BF16).T
+                dq[:, h * HEAD_DIM : (h + 1) * HEAD_DIM] = (gq * SCALE).astype(BF16).T
         dk1 = dk1 * SCALE
         own[0, :, cols] = dk1[:SHARD].astype(BF16)
         own[1, :, cols] = dv1[:SHARD].astype(BF16)
@@ -246,6 +301,14 @@
         drv[:HALF, cols] = dv1[SHARD:].astype(BF16)
         drk[HALF:, cols] = (dk2 * SCALE).astype(BF16)
         drv[HALF:, cols] = dv2.astype(BF16)
+        wide = pl.ds(g * GROUP_HEADS * HEAD_DIM, GROUP_HEADS * HEAD_DIM)
+        narrow = pl.ds(g * HEAD_DIM, HEAD_DIM)
+        send(out, out_hbm, wide)
+        send(dq, dq_hbm, wide)
+        send(drk, drk_hbm, narrow)
+        send(drv, drv_hbm, narrow)
+    for copy in started:
+        copy.wait()
 
 
 def add_partials(a, b, c, d, keys, values):
@@ -265,12 +328,13 @@
     return pltpu.with_memory_space_constraint(x, pltpu.HBM)
 
 
-def call(body, name, ins, outs, scratch=(), in_space=pltpu.VMEM, flops=0):
+def call(body, name, ins, outs, scratch=(), in_space=pltpu.VMEM, to_hbm=0, flops=0):
     return pl.pallas_call(
         body,
         name=name,
         in_specs=[pl.BlockSpec(memory_space=in_space)] * len(ins),
-        out_specs=[pl.BlockSpec(memory_space=pltpu.VMEM)] * len(outs),
+        out_specs=[pl.BlockSpec(memory_space=pltpu.HBM)] * to_hbm
+        + [pl.BlockSpec(memory_space=pltpu.VMEM)] * (len(outs) - to_hbm),
         out_shape=outs,
         scratch_shapes=list(scratch),
         cost_estimate=pl.CostEstimate(flops=flops, bytes_accessed=1 << 20, transcendentals=0),
@@ -292,7 +356,7 @@
         route = [(i, (i + steps * stride) % devices) for i in range(devices)]
         return lax.ppermute(block, "rows", route)
 
-    remote = [moved(stacked, steps) for steps in (1, 3, 2)]
+    remote = [moved(stacked, steps) for steps in STEPS]
     slot = row_slot.reshape(1, ROWS)
     pos = row_pos.reshape(1, ROWS)
     pair_heads = QUERY_HEADS // 2
@@ -323,29 +387,34 @@
                 VM((ROWS, ROWS), F32),
                 VM((1, ROWS), jnp.int32),
                 VM((1, ROWS), jnp.int32),
-                pltpu.SemaphoreType.DMA((6 + 2 * KV_HEADS,)),
+                pltpu.SemaphoreType.DMA((6 + QUERY_HEADS,)),
             ],
             in_space=pltpu.HBM,
             flops=10**9,
         ),
     )
     partial = (2, SHARD, width)
-    w, ds, f, d, g1, g2, g3 = call(
-        remote_pass,
-        "remote_pass",
-        [q, do, *remote, live, m, l, c],
-        [
-            VM((QUERY_HEADS, REMOTE, ROWS), BF16),
-            VM((QUERY_HEADS, REMOTE, ROWS), BF16),
-            VM(heads, F32),
-            VM(heads, F32),
-            hbm(partial, BF16),
-            hbm(partial, BF16),
-            hbm(partial, BF16),
-        ],
-        flops=2 * 10**9,
-    )
-    back = [moved(g, -steps) for g, steps in ((g1, 1), (g2, 3), (g3, 2))]
+    rx, ry, rz = remote
+    early = (QUERY_HEADS, 2 * SHARD, ROWS)
+    every = (QUERY_HEADS, ROWS // HALF, REMOTE, HALF)
+    e, p, tx, ty, m2, l2, c2 = map(
+        in_vmem,
+        call(
+            early_forward,
+            "early_forward",
+            [q, do, rx, ry, m, l, c],
+            [VM(early, F32)] * 2 + [VM(heads, F32)] * 5,
+            flops=10**9,
+        ),
+    )
+    w, ds, f, d, *terms = call(
+        late_pass,
+        "late_pass",
+        [q, do, rz, live, m, tx, ty, m2, l2, c2, e, p],
+        [VM(every, BF16)] * 2 + [VM(heads, F32)] * 2 + [hbm(partial, BF16)] * 3,
+        flops=10**9,
+    )
+    back = [moved(terms[n], -STEPS[n]) for n in SEND_ORDER]
     out, dq, drk, drv, own = call(
         local_backward,
         "local_backward",
@@ -357,7 +426,15 @@
             hbm(response_keys.shape, BF16),
             hbm(partial, BF16),
         ],
-        flops=3 * 10**9,
+        [
+            VM(query.shape, BF16),
+            VM(query.shape, BF16),
+            VM(response_keys.shape, BF16),
+            VM(response_keys.shape, BF16),
+            pltpu.SemaphoreType.DMA((4 * KV_HEADS,)),
+        ],
+        to_hbm=4,
+        flops=10**6,
     )
     gpk, gpv = call(
         add_partials,

time: 29.2 us -> 26.4 us (0.904)
  waiting for transfers between devices: 3.03 us -> 0.48 us
  Pallas kernels: 14.5 us -> 13.6 us
  starting transfers between devices: 9.73 us -> 10.3 us
    ppermute x6, waiting for transfers between devices: 3.03 us -> 0.48 us  [moved(): return lax.ppermute(block, 'rows', route)]
    pallas_call x4 -> x5, Pallas kernels: 14.5 us -> 13.6 us  [call(): pl.pallas_call(body, name=name, in_specs=[pl.BlockSpec(memory_space=in_sp...]
    ppermute x6, starting transfers between devices: 9.73 us -> 10.3 us  [moved(): return lax.ppermute(block, 'rows', route)]
  transfers between devices with their start and end apart: 6 -> 6, of which waited for: 3 -> 1; matrix products, arithmetic and copies ran while one was open for 0% -> 0% of each run, Pallas kernels for 31% -> 38%
where the time goes in v2:
time: 26.4 us; the launch traced here: 25.9 us
  Pallas kernels  13.6 us (52%)
  starting transfers between devices  10.3 us (39%)
  other arithmetic  0.89 us (3%)
  between operations  0.7 us (3%)
  waiting for transfers between devices  0.48 us (2%)
    pallas_call x5, Pallas kernels, call(): pl.pallas_call(body, name=name, in_specs=[pl.BlockSpec(memory_space=in_sp...  13.6 us
    ppermute x6, starting transfers between devices, moved(): return lax.ppermute(block, 'rows', route)  10.3 us
    another operation x1, other arithmetic, per_device(): stacked = jnp.stack([prompt_keys, prompt_values])  0.89 us
  transfers between devices with their start and end apart: 6, of which 1 were waited for; matrix products, arithmetic and copies ran while one was open for 0% of the time, Pallas kernels for 38%

profile of v2, /device:TPU:96, one launch (start us, length us, event | category | flops | bytes accessed | tf_op | source)
XLA Modules:
  0.0 25.9 jit_solution(1702646089712167093)
XLA Ops:
  0.6 0.9 %pad_maximum_fusion = bf16[2,128,256]{2,1,0:T(8,128)(2,1)S(1)} fusion(bf16[1,128,256]{2,1,0:T(8,128)(2,1)} %bitcast.5, bf16[1,128,256]{2,1,0:T(8,128)(2,1)} %bitcast.4), kind=kLoop, calls=%fused_computation | loop fusion | flops 65536 | bytes 262144 | tf_op jit(solution)/shard_map/stack | solution.py:353
  1.5 1.7 %collective-permute-start.1 = (bf16[2,128,256]{2,1,0:T(8,128)(2,1)S(1)}, bf16[2,128,256]{2,1,0:T(8,128)(2,1)S(1)}, u32[]{:S(2)}, u32[]{:S(2)}) collective-permute-start(bf16[2,128,256]{2,1,0:T(8,128)(2,1)S(1)} %pad_maximum_fusion), channel_id=1, source_target_pairs={{0,64},{1,65},{2,66},{3,67},{4,68},{5,69},{6,70},{7,71},{8,72},{9,... | collective-permute-start | bytes 393224 | tf_op jit(solution)/shard_map/ppermute | solution.py:357
  3.2 1.7 %collective-permute-start = (bf16[2,128,256]{2,1,0:T(8,128)(2,1)S(1)}, bf16[2,128,256]{2,1,0:T(8,128)(2,1)S(1)}, u32[]{:S(2)}, u32[]{:S(2)}) collective-permute-start(bf16[2,128,256]{2,1,0:T(8,128)(2,1)S(1)} %pad_maximum_fusion), channel_id=1, source_target_pairs={{0,192},{1,193},{2,194},{3,195},{4,196},{5,197},{6,198},{7,199},{8... | collective-permute-start | bytes 393224 | tf_op jit(solution)/shard_map/ppermute | solution.py:357
  4.8 2.0 %collective-permute-start.2 = (bf16[2,128,256]{2,1,0:T(8,128)(2,1)S(1)}, bf16[2,128,256]{2,1,0:T(8,128)(2,1)S(1)}, u32[]{:S(2)}, u32[]{:S(2)}) collective-permute-start(bf16[2,128,256]{2,1,0:T(8,128)(2,1)S(1)} %pad_maximum_fusion), channel_id=1, source_target_pairs={{0,128},{1,129},{2,130},{3,131},{4,132},{5,133},{6,134},{7,135},{8... | collective-permute-start | bytes 393224 | tf_op jit(solution)/shard_map/ppermute | solution.py:357
  6.8 3.7 %local_forward.1 = (bf16[256,2048]{1,0:T(8,128)(2,1)S(1)}, bf16[256,2048]{1,0:T(8,128)(2,1)S(1)}, bf16[2,384,256]{2,1,0:T(8,128)(2,1)S(1)}, f32[16,256,256]{2,1,...) custom-call(bf16[256,2048]{1,0:T(8,128)(2,1)} %q_in.1, ...), custom_call_target="tpu_custom_call" | custom-call | flops 1000000000 | bytes 1048576 | tf_op jit(solution)/shard_map/local_forward/pallas_call | solution.py:332
  10.5 0.0 collective-permute-done.1.ry
  10.5 0.0 collective-permute-done.rx
  10.5 1.7 %early_forward.1 = (f32[16,256,256]{2,1,0:T(8,128)S(1)}, f32[16,256,256]{2,1,0:T(8,128)S(1)}, f32[16,256]{1,0:T(8,128)S(1)}, f32[16,256]{1,0:T(8,128)S(1)}, f32[...) custom-call(bf16[256,2048]{1,0:T(8,128)(2,1)S(1)} %get-tuple-element.38.q, ...), custom_call_target="tpu_custom_call" | custom-call | flops 1000000000 | bytes 1048576 | tf_op jit(solution)/shard_map/early_forward/pallas_call | solution.py:332
  12.2 0.0 collective-permute-done.2.rz
  12.2 2.9 %late_pass.1 = (bf16[16,2,384,128]{3,2,1,0:T(8,128)(2,1)S(1)}, bf16[16,2,384,128]{3,2,1,0:T(8,128)(2,1)S(1)}, f32[16,256]{1,0:T(8,128)S(1)}, f32[16,256]{1,0:T(8...) custom-call(bf16[256,2048]{1,0:T(8,128)(2,1)S(1)} %get-tuple-element, ...), custom_call_target="tpu_custom_call" | custom-call | flops 1000000000 | bytes 1048576 | tf_op jit(solution)/shard_map/late_pass/pallas_call | solution.py:332
  15.2 1.1 %collective-permute-start.3 = (bf16[2,128,256]{2,1,0:T(8,128)(2,1)S(1)}, bf16[2,128,256]{2,1,0:T(8,128)(2,1)S(1)}, u32[]{:S(2)}, u32[]{:S(2)}) collective-permute-start(bf16[2,128,256]{2,1,0:T(8,128)(2,1)S(1)} %get-tuple-element.65), channel_id=1, source_target_pairs={{0,64},{1,65},{2,66},{3,67},{4,68},{5,69},{6,70},{7,71},{8,72},{9,... | collective-permute-start | bytes 393224 | tf_op jit(solution)/shard_map/ppermute | solution.py:357
  16.3 2.5 %collective-permute-start.4 = (bf16[2,128,256]{2,1,0:T(8,128)(2,1)S(1)}, bf16[2,128,256]{2,1,0:T(8,128)(2,1)S(1)}, u32[]{:S(2)}, u32[]{:S(2)}) collective-permute-start(bf16[2,128,256]{2,1,0:T(8,128)(2,1)S(1)} %get-tuple-element.66), channel_id=1, source_target_pairs={{0,192},{1,193},{2,194},{3,195},{4,196},{5,197},{6,198},{7,199},{8... | collective-permute-start | bytes 393224 | tf_op jit(solution)/shard_map/ppermute | solution.py:357
  18.8 1.4 %collective-permute-start.5 = (bf16[2,128,256]{2,1,0:T(8,128)(2,1)S(1)}, bf16[2,128,256]{2,1,0:T(8,128)(2,1)S(1)}, u32[]{:S(2)}, u32[]{:S(2)}) collective-permute-start(bf16[2,128,256]{2,1,0:T(8,128)(2,1)S(1)} %get-tuple-element.67), channel_id=1, source_target_pairs={{0,128},{1,129},{2,130},{3,131},{4,132},{5,133},{6,134},{7,135},{8... | collective-permute-start | bytes 393224 | tf_op jit(solution)/shard_map/ppermute | solution.py:357
  20.1 4.6 %local_backward.1 = (bf16[256,2048]{1,0:T(8,128)(2,1)}, bf16[256,2048]{1,0:T(8,128)(2,1)}, bf16[256,256]{1,0:T(8,128)(2,1)}, bf16[256,256]{1,0:T(8,128)(2,1)}, bf16[2,128,256]{2,1,0:T(8,128)(2,1)S(1)}) custom-call(bf16[256,2048]{1,0:T(8,128)(2,1)S(1)} %get-tuple-element.38.q, bf16[256,2048]{1,0:T(8,128)(2,1)S(1)} %get-tuple-element.39.do, ...), custom_call_target="tpu_custom_call" | custom-call | flops 1000000 | bytes 1048576 | tf_op jit(solution)/shard_map/local_backward/pallas_call | solution.py:332
  24.8 0.0 collective-permute-done.3.b
  24.8 0.0 collective-permute-done.4.c
  24.8 0.5 %collective-permute-done.5.d = bf16[2,128,256]{2,1,0:T(8,128)(2,1)S(1)} collective-permute-done((bf16[2,128,256]{2,1,0:T(8,128)(2,1)S(1)}, bf16[2,128,256]{2,1,0:T(8,128)(2,1)S(1)}, u32[]{:S(2)}, u32[]{:S(2)}) %collective-permute-start.5) | collective-permute-done | bytes 131104 | tf_op jit(solution)/shard_map/ppermute | solution.py:357
  25.2 0.7 %add_partials.1 = (bf16[128,256]{1,0:T(8,128)(2,1)}, bf16[128,256]{1,0:T(8,128)(2,1)}) custom-call(bf16[2,128,256]{2,1,0:T(8,128)(2,1)S(1)} %get-tuple-element.64.a, bf16[2,128,256]{2,1,0:T(8,128)(2,1)S(1)} %collective-permute-done.3.b, bf16[2,128,256]{2,1,0:T(8,128)(2,1)S(1)} %collective-permute-done.4.c, bf16[2,128,256]{2,1,0:T(8,128)(2,1)S(1)} %collective-permute-done.5.d), custom_call_target="tpu_custom_call" | custom-call | bytes 1048576 | tf_op jit(solution)/shard_map/add_partials/pallas_call | solution.py:332
Async XLA Ops:
  1.5 9.0 %collective-permute-start.1 = (bf16[2,128,256]{2,1,0:T(8,128)(2,1)S(1)}, bf16[2,128,256]{2,1,0:T(8,128)(2,1)S(1)}, u32[]{:S(2)}, u32[]{:S(2)}) collective-permute-start(bf16[2,128,256]{2,1,0:T(8,128)(2,1)S(1)} %pad_maximum_fusion), channel_id=1, source_target_pairs={{0,64},{1,65},{2,66},{3,67},{4,68},{5,69},{6,70},{7,71},{8,72},{9,... | collective-permute-start | bytes 393224 | tf_op jit(solution)/shard_map/ppermute | solution.py:357
  3.2 7.3 %collective-permute-start = (bf16[2,128,256]{2,1,0:T(8,128)(2,1)S(1)}, bf16[2,128,256]{2,1,0:T(8,128)(2,1)S(1)}, u32[]{:S(2)}, u32[]{:S(2)}) collective-permute-start(bf16[2,128,256]{2,1,0:T(8,128)(2,1)S(1)} %pad_maximum_fusion), channel_id=1, source_target_pairs={{0,192},{1,193},{2,194},{3,195},{4,196},{5,197},{6,198},{7,199},{8... | collective-permute-start | bytes 393224 | tf_op jit(solution)/shard_map/ppermute | solution.py:357
  4.8 7.4 %collective-permute-start.2 = (bf16[2,128,256]{2,1,0:T(8,128)(2,1)S(1)}, bf16[2,128,256]{2,1,0:T(8,128)(2,1)S(1)}, u32[]{:S(2)}, u32[]{:S(2)}) collective-permute-start(bf16[2,128,256]{2,1,0:T(8,128)(2,1)S(1)} %pad_maximum_fusion), channel_id=1, source_target_pairs={{0,128},{1,129},{2,130},{3,131},{4,132},{5,133},{6,134},{7,135},{8... | collective-permute-start | bytes 393224 | tf_op jit(solution)/shard_map/ppermute | solution.py:357
  15.2 9.6 %collective-permute-start.3 = (bf16[2,128,256]{2,1,0:T(8,128)(2,1)S(1)}, bf16[2,128,256]{2,1,0:T(8,128)(2,1)S(1)}, u32[]{:S(2)}, u32[]{:S(2)}) collective-permute-start(bf16[2,128,256]{2,1,0:T(8,128)(2,1)S(1)} %get-tuple-element.65), channel_id=1, source_target_pairs={{0,64},{1,65},{2,66},{3,67},{4,68},{5,69},{6,70},{7,71},{8,72},{9,... | collective-permute-start | bytes 393224 | tf_op jit(solution)/shard_map/ppermute | solution.py:357
  16.3 8.5 %collective-permute-start.4 = (bf16[2,128,256]{2,1,0:T(8,128)(2,1)S(1)}, bf16[2,128,256]{2,1,0:T(8,128)(2,1)S(1)}, u32[]{:S(2)}, u32[]{:S(2)}) collective-permute-start(bf16[2,128,256]{2,1,0:T(8,128)(2,1)S(1)} %get-tuple-element.66), channel_id=1, source_target_pairs={{0,192},{1,193},{2,194},{3,195},{4,196},{5,197},{6,198},{7,199},{8... | collective-permute-start | bytes 393224 | tf_op jit(solution)/shard_map/ppermute | solution.py:357
  18.8 6.5 %collective-permute-start.5 = (bf16[2,128,256]{2,1,0:T(8,128)(2,1)S(1)}, bf16[2,128,256]{2,1,0:T(8,128)(2,1)S(1)}, u32[]{:S(2)}, u32[]{:S(2)}) collective-permute-start(bf16[2,128,256]{2,1,0:T(8,128)(2,1)S(1)} %get-tuple-element.67), channel_id=1, source_target_pairs={{0,128},{1,129},{2,130},{3,131},{4,132},{5,133},{6,134},{7,135},{8... | collective-permute-start | bytes 393224 | tf_op jit(solution)/shard_map/ppermute | solution.py:357

commit v3 on v2

--- a/solution.py
+++ b/solution.py
@@ -67,10 +67,10 @@
         (pv, kv.at[1, pl.ds(0, SHARD)]),
         (rv, kv.at[1, pl.ds(SHARD, ROWS)]),
     ]
-    for n in range(QUERY_HEADS // 2):
-        span = pl.ds(n * 2 * HEAD_DIM, 2 * HEAD_DIM)
-        pieces.append((q_in.at[:, span], q.at[:, span]))
-        pieces.append((do_in.at[:, span], do.at[:, span]))
+    for h in range(QUERY_HEADS):
+        span = pl.ds(h * HEAD_DIM, HEAD_DIM)
+        pieces.append((q_in.at[:, span], q.at[h]))
+        pieces.append((do_in.at[:, span], do.at[h]))
     copies = [pltpu.make_async_copy(a, b, sems.at[n]) for n, (a, b) in enumerate(pieces)]
     for copy in copies:
         copy.start()
@@ -98,10 +98,10 @@
             first = g * GROUP_HEADS + 2 * pair
             if first in LOAD_AT:
                 stop = min([n for n in LOAD_AT if n > first] + [QUERY_HEADS])
-                for copy in copies[6 + first : 6 + stop]:
+                for copy in copies[6 + 2 * first : 6 + 2 * stop]:
                     copy.wait()
-            qs = [q[:, h * HEAD_DIM : (h + 1) * HEAD_DIM] for h in (first, first + 1)]
-            ds = [do[:, h * HEAD_DIM : (h + 1) * HEAD_DIM] for h in (first, first + 1)]
+            qs = [head(q, h) for h in (first, first + 1)]
+            ds = [head(do, h) for h in (first, first + 1)]
             b2 = bias[HALF:, HALF:]
             s2 = dot_nt(k2, second_half(*qs)) + jnp.concatenate([b2, b2], axis=1)
             m2 = col_max(s2)
@@ -131,7 +131,7 @@
 
 
 def head(ref, h):
-    return ref[:, h * HEAD_DIM : (h + 1) * HEAD_DIM]
+    return ref[h]
 
 
 def columns_of(h):
@@ -271,8 +271,8 @@
         dv2 = jnp.zeros((HALF, HEAD_DIM), F32)
         for pair in range(GROUP_HEADS // 2):
             first = g * GROUP_HEADS + 2 * pair
-            qs = [q[:, h * HEAD_DIM : (h + 1) * HEAD_DIM] for h in (first, first + 1)]
-            ds = [do[:, h * HEAD_DIM : (h + 1) * HEAD_DIM] for h in (first, first + 1)]
+            qs = [head(q, h) for h in (first, first + 1)]
+            ds = [head(do, h) for h in (first, first + 1)]
             fs = [f_in[h : h + 1, :] for h in (first, first + 1)]
             cs = [d_in[h : h + 1, :] for h in (first, first + 1)]
             w2 = p2[first // 2] * halves(*fs)
@@ -371,8 +371,8 @@
             "local_forward",
             [in_hbm(x) for x in arrays],
             [
-                VM(query.shape, BF16),
-                VM(query.shape, BF16),
+                VM((QUERY_HEADS, ROWS, HEAD_DIM), BF16),
+                VM((QUERY_HEADS, ROWS, HEAD_DIM), BF16),
                 VM((2, SHARD + ROWS, width), BF16),
                 VM((QUERY_HEADS, near, ROWS), F32),
                 VM((QUERY_HEADS, near, ROWS), F32),
@@ -387,7 +387,7 @@
                 VM((ROWS, ROWS), F32),
                 VM((1, ROWS), jnp.int32),
                 VM((1, ROWS), jnp.int32),
-                pltpu.SemaphoreType.DMA((6 + QUERY_HEADS,)),
+                pltpu.SemaphoreType.DMA((6 + 2 * QUERY_HEADS,)),
             ],
             in_space=pltpu.HBM,
             flops=10**9,

time: 26.4 us -> 25.9 us (0.981); the launches traced: 25.9 us -> 25.8 us
  Pallas kernels: 13.6 us -> 13.2 us
  waiting for transfers between devices: 0.48 us -> 0.77 us
    pallas_call x5, Pallas kernels: 13.6 us -> 13.2 us  [call(): pl.pallas_call(body, name=name, in_specs=[pl.BlockSpec(memory_space=in_sp...]
    ppermute x6, waiting for transfers between devices: 0.48 us -> 0.77 us  [moved(): return lax.ppermute(block, 'rows', route)]
where the time goes in v3:
time: 25.9 us; the launch traced here: 25.8 us
  Pallas kernels  13.2 us (51%)
  starting transfers between devices  10.2 us (39%)
  other arithmetic  0.89 us (3%)
  waiting for transfers between devices  0.77 us (3%)
  between operations  0.7 us (3%)
    pallas_call x5, Pallas kernels, call(): pl.pallas_call(body, name=name, in_specs=[pl.BlockSpec(memory_space=in_sp...  13.2 us
    ppermute x6, starting transfers between devices, moved(): return lax.ppermute(block, 'rows', route)  10.2 us
    another operation x1, other arithmetic, per_device(): stacked = jnp.stack([prompt_keys, prompt_values])  0.89 us
    ppermute x6, waiting for transfers between devices, moved(): return lax.ppermute(block, 'rows', route)  0.77 us
  transfers between devices with their start and end apart: 6, of which 1 were waited for; matrix products, arithmetic and copies ran while one was open for 0% of the time, Pallas kernels for 38%

profile of v3, /device:TPU:96, one launch (start us, length us, event | category | flops | bytes accessed | tf_op | source)
XLA Modules:
  0.0 25.8 jit_solution(14407451551153034687)
XLA Ops:
  0.6 0.9 %pad_maximum_fusion = bf16[2,128,256]{2,1,0:T(8,128)(2,1)S(1)} fusion(bf16[1,128,256]{2,1,0:T(8,128)(2,1)} %bitcast.5, bf16[1,128,256]{2,1,0:T(8,128)(2,1)} %bitcast.4), kind=kLoop, calls=%fused_computation | loop fusion | flops 65536 | bytes 262144 | tf_op jit(solution)/shard_map/stack | solution.py:353
  1.5 1.7 %collective-permute-start.1 = (bf16[2,128,256]{2,1,0:T(8,128)(2,1)S(1)}, bf16[2,128,256]{2,1,0:T(8,128)(2,1)S(1)}, u32[]{:S(2)}, u32[]{:S(2)}) collective-permute-start(bf16[2,128,256]{2,1,0:T(8,128)(2,1)S(1)} %pad_maximum_fusion), channel_id=1, source_target_pairs={{0,64},{1,65},{2,66},{3,67},{4,68},{5,69},{6,70},{7,71},{8,72},{9,... | collective-permute-start | bytes 393224 | tf_op jit(solution)/shard_map/ppermute | solution.py:357
  3.2 1.7 %collective-permute-start = (bf16[2,128,256]{2,1,0:T(8,128)(2,1)S(1)}, bf16[2,128,256]{2,1,0:T(8,128)(2,1)S(1)}, u32[]{:S(2)}, u32[]{:S(2)}) collective-permute-start(bf16[2,128,256]{2,1,0:T(8,128)(2,1)S(1)} %pad_maximum_fusion), channel_id=1, source_target_pairs={{0,192},{1,193},{2,194},{3,195},{4,196},{5,197},{6,198},{7,199},{8... | collective-permute-start | bytes 393224 | tf_op jit(solution)/shard_map/ppermute | solution.py:357
  4.8 2.0 %collective-permute-start.2 = (bf16[2,128,256]{2,1,0:T(8,128)(2,1)S(1)}, bf16[2,128,256]{2,1,0:T(8,128)(2,1)S(1)}, u32[]{:S(2)}, u32[]{:S(2)}) collective-permute-start(bf16[2,128,256]{2,1,0:T(8,128)(2,1)S(1)} %pad_maximum_fusion), channel_id=1, source_target_pairs={{0,128},{1,129},{2,130},{3,131},{4,132},{5,133},{6,134},{7,135},{8... | collective-permute-start | bytes 393224 | tf_op jit(solution)/shard_map/ppermute | solution.py:357
  6.8 3.7 %local_forward.1 = (bf16[16,256,128]{2,1,0:T(8,128)(2,1)S(1)}, bf16[16,256,128]{2,1,0:T(8,128)(2,1)S(1)}, bf16[2,384,256]{2,1,0:T(8,128)(2,1)S(1)}, f32[16,256,2...) custom-call(bf16[256,2048]{1,0:T(8,128)(2,1)} %q_in.1, ...), custom_call_target="tpu_custom_call" | custom-call | flops 1000000000 | bytes 1048576 | tf_op jit(solution)/shard_map/local_forward/pallas_call | solution.py:332
  10.5 0.0 collective-permute-done.1.ry
  10.5 0.0 collective-permute-done.rx
  10.5 1.5 %early_forward.1 = (f32[16,256,256]{2,1,0:T(8,128)S(1)}, f32[16,256,256]{2,1,0:T(8,128)S(1)}, f32[16,256]{1,0:T(8,128)S(1)}, f32[16,256]{1,0:T(8,128)S(1)}, f32[...) custom-call(bf16[16,256,128]{2,1,0:T(8,128)(2,1)S(1)} %get-tuple-element.38.q, ...), custom_call_target="tpu_custom_call" | custom-call | flops 1000000000 | bytes 1048576 | tf_op jit(solution)/shard_map/early_forward/pallas_call | solution.py:332
  12.0 0.0 collective-permute-done.2.rz
  12.1 2.7 %late_pass.1 = (bf16[16,2,384,128]{3,2,1,0:T(8,128)(2,1)S(1)}, bf16[16,2,384,128]{3,2,1,0:T(8,128)(2,1)S(1)}, f32[16,256]{1,0:T(8,128)S(1)}, f32[16,256]{1,0:T(8...) custom-call(bf16[16,256,128]{2,1,0:T(8,128)(2,1)S(1)} %get-tuple-ele, ...), custom_call_target="tpu_custom_call" | custom-call | flops 1000000000 | bytes 1048576 | tf_op jit(solution)/shard_map/late_pass/pallas_call | solution.py:332
  14.8 1.2 %collective-permute-start.3 = (bf16[2,128,256]{2,1,0:T(8,128)(2,1)S(1)}, bf16[2,128,256]{2,1,0:T(8,128)(2,1)S(1)}, u32[]{:S(2)}, u32[]{:S(2)}) collective-permute-start(bf16[2,128,256]{2,1,0:T(8,128)(2,1)S(1)} %get-tuple-element.65), channel_id=1, source_target_pairs={{0,64},{1,65},{2,66},{3,67},{4,68},{5,69},{6,70},{7,71},{8,72},{9,... | collective-permute-start | bytes 393224 | tf_op jit(solution)/shard_map/ppermute | solution.py:357
  16.1 2.3 %collective-permute-start.4 = (bf16[2,128,256]{2,1,0:T(8,128)(2,1)S(1)}, bf16[2,128,256]{2,1,0:T(8,128)(2,1)S(1)}, u32[]{:S(2)}, u32[]{:S(2)}) collective-permute-start(bf16[2,128,256]{2,1,0:T(8,128)(2,1)S(1)} %get-tuple-element.66), channel_id=1, source_target_pairs={{0,192},{1,193},{2,194},{3,195},{4,196},{5,197},{6,198},{7,199},{8... | collective-permute-start | bytes 393224 | tf_op jit(solution)/shard_map/ppermute | solution.py:357
  18.4 1.4 %collective-permute-start.5 = (bf16[2,128,256]{2,1,0:T(8,128)(2,1)S(1)}, bf16[2,128,256]{2,1,0:T(8,128)(2,1)S(1)}, u32[]{:S(2)}, u32[]{:S(2)}) collective-permute-start(bf16[2,128,256]{2,1,0:T(8,128)(2,1)S(1)} %get-tuple-element.67), channel_id=1, source_target_pairs={{0,128},{1,129},{2,130},{3,131},{4,132},{5,133},{6,134},{7,135},{8... | collective-permute-start | bytes 393224 | tf_op jit(solution)/shard_map/ppermute | solution.py:357
  19.8 4.6 %local_backward.1 = (bf16[256,2048]{1,0:T(8,128)(2,1)}, bf16[256,2048]{1,0:T(8,128)(2,1)}, bf16[256,256]{1,0:T(8,128)(2,1)}, bf16[256,256]{1,0:T(8,128)(2,1)}, bf16[2,128,256]{2,1,0:T(8,128)(2,1)S(1)}) custom-call(bf16[16,256,128]{2,1,0:T(8,128)(2,1)S(1)} %get-tuple-element.38.q, bf16[16,256,128]{2,1,0:T(8,128)(2,1)S(1)} %get-tuple-element.39.do, ...), custom_call_target="tpu_custom_call" | custom-call | flops 1000000 | bytes 1048576 | tf_op jit(solution)/shard_map/local_backward/pallas_call | solution.py:332
  24.3 0.0 collective-permute-done.3.b
  24.3 0.0 collective-permute-done.4.c
  24.4 0.7 %collective-permute-done.5.d = bf16[2,128,256]{2,1,0:T(8,128)(2,1)S(1)} collective-permute-done((bf16[2,128,256]{2,1,0:T(8,128)(2,1)S(1)}, bf16[2,128,256]{2,1,0:T(8,128)(2,1)S(1)}, u32[]{:S(2)}, u32[]{:S(2)}) %collective-permute-start.5) | collective-permute-done | bytes 131104 | tf_op jit(solution)/shard_map/ppermute | solution.py:357
  25.1 0.7 %add_partials.1 = (bf16[128,256]{1,0:T(8,128)(2,1)}, bf16[128,256]{1,0:T(8,128)(2,1)}) custom-call(bf16[2,128,256]{2,1,0:T(8,128)(2,1)S(1)} %get-tuple-element.64.a, bf16[2,128,256]{2,1,0:T(8,128)(2,1)S(1)} %collective-permute-done.3.b, bf16[2,128,256]{2,1,0:T(8,128)(2,1)S(1)} %collective-permute-done.4.c, bf16[2,128,256]{2,1,0:T(8,128)(2,1)S(1)} %collective-permute-done.5.d), custom_call_target="tpu_custom_call" | custom-call | bytes 1048576 | tf_op jit(solution)/shard_map/add_partials/pallas_call | solution.py:332
Async XLA Ops:
  1.5 9.0 %collective-permute-start.1 = (bf16[2,128,256]{2,1,0:T(8,128)(2,1)S(1)}, bf16[2,128,256]{2,1,0:T(8,128)(2,1)S(1)}, u32[]{:S(2)}, u32[]{:S(2)}) collective-permute-start(bf16[2,128,256]{2,1,0:T(8,128)(2,1)S(1)} %pad_maximum_fusion), channel_id=1, source_target_pairs={{0,64},{1,65},{2,66},{3,67},{4,68},{5,69},{6,70},{7,71},{8,72},{9,... | collective-permute-start | bytes 393224 | tf_op jit(solution)/shard_map/ppermute | solution.py:357
  3.2 7.4 %collective-permute-start = (bf16[2,128,256]{2,1,0:T(8,128)(2,1)S(1)}, bf16[2,128,256]{2,1,0:T(8,128)(2,1)S(1)}, u32[]{:S(2)}, u32[]{:S(2)}) collective-permute-start(bf16[2,128,256]{2,1,0:T(8,128)(2,1)S(1)} %pad_maximum_fusion), channel_id=1, source_target_pairs={{0,192},{1,193},{2,194},{3,195},{4,196},{5,197},{6,198},{7,199},{8... | collective-permute-start | bytes 393224 | tf_op jit(solution)/shard_map/ppermute | solution.py:357
  4.8 7.3 %collective-permute-start.2 = (bf16[2,128,256]{2,1,0:T(8,128)(2,1)S(1)}, bf16[2,128,256]{2,1,0:T(8,128)(2,1)S(1)}, u32[]{:S(2)}, u32[]{:S(2)}) collective-permute-start(bf16[2,128,256]{2,1,0:T(8,128)(2,1)S(1)} %pad_maximum_fusion), channel_id=1, source_target_pairs={{0,128},{1,129},{2,130},{3,131},{4,132},{5,133},{6,134},{7,135},{8... | collective-permute-start | bytes 393224 | tf_op jit(solution)/shard_map/ppermute | solution.py:357
  14.8 9.5 %collective-permute-start.3 = (bf16[2,128,256]{2,1,0:T(8,128)(2,1)S(1)}, bf16[2,128,256]{2,1,0:T(8,128)(2,1)S(1)}, u32[]{:S(2)}, u32[]{:S(2)}) collective-permute-start(bf16[2,128,256]{2,1,0:T(8,128)(2,1)S(1)} %get-tuple-element.65), channel_id=1, source_target_pairs={{0,64},{1,65},{2,66},{3,67},{4,68},{5,69},{6,70},{7,71},{8,72},{9,... | collective-permute-start | bytes 393224 | tf_op jit(solution)/shard_map/ppermute | solution.py:357
  16.1 8.3 %collective-permute-start.4 = (bf16[2,128,256]{2,1,0:T(8,128)(2,1)S(1)}, bf16[2,128,256]{2,1,0:T(8,128)(2,1)S(1)}, u32[]{:S(2)}, u32[]{:S(2)}) collective-permute-start(bf16[2,128,256]{2,1,0:T(8,128)(2,1)S(1)} %get-tuple-element.66), channel_id=1, source_target_pairs={{0,192},{1,193},{2,194},{3,195},{4,196},{5,197},{6,198},{7,199},{8... | collective-permute-start | bytes 393224 | tf_op jit(solution)/shard_map/ppermute | solution.py:357
  18.4 6.7 %collective-permute-start.5 = (bf16[2,128,256]{2,1,0:T(8,128)(2,1)S(1)}, bf16[2,128,256]{2,1,0:T(8,128)(2,1)S(1)}, u32[]{:S(2)}, u32[]{:S(2)}) collective-permute-start(bf16[2,128,256]{2,1,0:T(8,128)(2,1)S(1)} %get-tuple-element.67), channel_id=1, source_target_pairs={{0,128},{1,129},{2,130},{3,131},{4,132},{5,133},{6,134},{7,135},{8... | collective-permute-start | bytes 393224 | tf_op jit(solution)/shard_map/ppermute | solution.py:357

commit v4 on v3

--- a/solution.py
+++ b/solution.py
@@ -62,11 +62,12 @@
     pieces = [
         (slot_in, slot),
         (pos_in, pos),
-        (pk, kv.at[0, pl.ds(0, SHARD)]),
-        (rk, kv.at[0, pl.ds(SHARD, ROWS)]),
-        (pv, kv.at[1, pl.ds(0, SHARD)]),
-        (rv, kv.at[1, pl.ds(SHARD, ROWS)]),
     ]
+    for g in range(KV_HEADS):
+        cols = pl.ds(g * HEAD_DIM, HEAD_DIM)
+        for n, (shard, rows) in enumerate(((pk, rk), (pv, rv))):
+            pieces.append((shard.at[:, cols], kv.at[n, g, pl.ds(0, SHARD)]))
+            pieces.append((rows.at[:, cols], kv.at[n, g, pl.ds(SHARD, ROWS)]))
     for h in range(QUERY_HEADS):
         span = pl.ds(h * HEAD_DIM, HEAD_DIM)
         pieces.append((q_in.at[:, span], q.at[h]))
@@ -86,19 +87,19 @@
     nothing = jnp.full((1, HALF), NEG, F32)
     zero = jnp.zeros((1, HALF), F32)
     near = SHARD + HALF
-    for copy in copies[2:6]:
+    for copy in copies[2:10]:
         copy.wait()
     for g in range(KV_HEADS):
         cols = slice(g * HEAD_DIM, (g + 1) * HEAD_DIM)
-        k1 = kv[0, :near, cols]
-        v1 = kv[1, :near, cols]
-        k2 = kv[0, near:, cols]
-        v2 = kv[1, near:, cols]
+        k1 = kv[0, g, :near]
+        v1 = kv[1, g, :near]
+        k2 = kv[0, g, near:]
+        v2 = kv[1, g, near:]
         for pair in range(GROUP_HEADS // 2):
             first = g * GROUP_HEADS + 2 * pair
             if first in LOAD_AT:
                 stop = min([n for n in LOAD_AT if n > first] + [QUERY_HEADS])
-                for copy in copies[6 + 2 * first : 6 + 2 * stop]:
+                for copy in copies[10 + 2 * first : 10 + 2 * stop]:
                     copy.wait()
             qs = [head(q, h) for h in (first, first + 1)]
             ds = [head(do, h) for h in (first, first + 1)]
@@ -260,10 +261,10 @@
         cols = slice(g * HEAD_DIM, (g + 1) * HEAD_DIM)
         shards = (rx, ry, rz)
         k_t = jnp.concatenate(
-            [kv[0, :near, cols]] + [r[0, :, cols] for r in shards] + [kv[0, near:, cols]], axis=0
+            [kv[0, g, :near]] + [r[0, :, cols] for r in shards] + [kv[0, g, near:]], axis=0
         ).T
         v_t = jnp.concatenate(
-            [kv[1, :near, cols]] + [r[1, :, cols] for r in shards] + [kv[1, near:, cols]], axis=0
+            [kv[1, g, :near]] + [r[1, :, cols] for r in shards] + [kv[1, g, near:]], axis=0
         ).T
         dk1 = jnp.zeros((near, HEAD_DIM), F32)
         dv1 = jnp.zeros((near, HEAD_DIM), F32)
@@ -373,7 +374,7 @@
             [
                 VM((QUERY_HEADS, ROWS, HEAD_DIM), BF16),
                 VM((QUERY_HEADS, ROWS, HEAD_DIM), BF16),
-                VM((2, SHARD + ROWS, width), BF16),
+                VM((2, KV_HEADS, SHARD + ROWS, HEAD_DIM), BF16),
                 VM((QUERY_HEADS, near, ROWS), F32),
                 VM((QUERY_HEADS, near, ROWS), F32),
                 VM((pair_heads, HALF, ROWS), F32),
@@ -387,7 +388,7 @@
                 VM((ROWS, ROWS), F32),
                 VM((1, ROWS), jnp.int32),
                 VM((1, ROWS), jnp.int32),
-                pltpu.SemaphoreType.DMA((6 + 2 * QUERY_HEADS,)),
+                pltpu.SemaphoreType.DMA((10 + 2 * QUERY_HEADS,)),
             ],
             in_space=pltpu.HBM,
             flops=10**9,

time: 25.9 us -> 26 us (level)
  no operation moved by 1% of the time
where the time goes in v4:
time: 26 us; the launch traced here: 25.8 us
  Pallas kernels  13.2 us (51%)
  starting transfers between devices  10.2 us (39%)
  other arithmetic  0.89 us (3%)
  waiting for transfers between devices  0.73 us (3%)
  between operations  0.7 us (3%)
    pallas_call x5, Pallas kernels, call(): pl.pallas_call(body, name=name, in_specs=[pl.BlockSpec(memory_space=in_sp...  13.2 us
    ppermute x6, starting transfers between devices, moved(): return lax.ppermute(block, 'rows', route)  10.2 us
    another operation x1, other arithmetic, per_device(): stacked = jnp.stack([prompt_keys, prompt_values])  0.89 us
    ppermute x6, waiting for transfers between devices, moved(): return lax.ppermute(block, 'rows', route)  0.73 us
  transfers between devices with their start and end apart: 6, of which 1 were waited for; matrix products, arithmetic and copies ran while one was open for 0% of the time, Pallas kernels for 38%

profile of v4, /device:TPU:96, one launch (start us, length us, event | category | flops | bytes accessed | tf_op | source)
XLA Modules:
  0.0 25.8 jit_solution(6592541975495643773)
XLA Ops:
  0.6 0.9 %pad_maximum_fusion = bf16[2,128,256]{2,1,0:T(8,128)(2,1)S(1)} fusion(bf16[1,128,256]{2,1,0:T(8,128)(2,1)} %bitcast.5, bf16[1,128,256]{2,1,0:T(8,128)(2,1)} %bitcast.4), kind=kLoop, calls=%fused_computation | loop fusion | flops 65536 | bytes 262144 | tf_op jit(solution)/shard_map/stack | solution.py:354
  1.5 1.7 %collective-permute-start.1 = (bf16[2,128,256]{2,1,0:T(8,128)(2,1)S(1)}, bf16[2,128,256]{2,1,0:T(8,128)(2,1)S(1)}, u32[]{:S(2)}, u32[]{:S(2)}) collective-permute-start(bf16[2,128,256]{2,1,0:T(8,128)(2,1)S(1)} %pad_maximum_fusion), channel_id=1, source_target_pairs={{0,64},{1,65},{2,66},{3,67},{4,68},{5,69},{6,70},{7,71},{8,72},{9,... | collective-permute-start | bytes 393224 | tf_op jit(solution)/shard_map/ppermute | solution.py:358
  3.2 1.7 %collective-permute-start = (bf16[2,128,256]{2,1,0:T(8,128)(2,1)S(1)}, bf16[2,128,256]{2,1,0:T(8,128)(2,1)S(1)}, u32[]{:S(2)}, u32[]{:S(2)}) collective-permute-start(bf16[2,128,256]{2,1,0:T(8,128)(2,1)S(1)} %pad_maximum_fusion), channel_id=1, source_target_pairs={{0,192},{1,193},{2,194},{3,195},{4,196},{5,197},{6,198},{7,199},{8... | collective-permute-start | bytes 393224 | tf_op jit(solution)/shard_map/ppermute | solution.py:358
  4.8 2.0 %collective-permute-start.2 = (bf16[2,128,256]{2,1,0:T(8,128)(2,1)S(1)}, bf16[2,128,256]{2,1,0:T(8,128)(2,1)S(1)}, u32[]{:S(2)}, u32[]{:S(2)}) collective-permute-start(bf16[2,128,256]{2,1,0:T(8,128)(2,1)S(1)} %pad_maximum_fusion), channel_id=1, source_target_pairs={{0,128},{1,129},{2,130},{3,131},{4,132},{5,133},{6,134},{7,135},{8... | collective-permute-start | bytes 393224 | tf_op jit(solution)/shard_map/ppermute | solution.py:358
  6.8 3.7 %local_forward.1 = (bf16[16,256,128]{2,1,0:T(8,128)(2,1)S(1)}, bf16[16,256,128]{2,1,0:T(8,128)(2,1)S(1)}, bf16[2,2,384,128]{3,2,1,0:T(8,128)(2,1)S(1)}, f32[16,2...) custom-call(bf16[256,2048]{1,0:T(8,128)(2,1)} %q_in.1, ...), custom_call_target="tpu_custom_call" | custom-call | flops 1000000000 | bytes 1048576 | tf_op jit(solution)/shard_map/local_forward/pallas_call | solution.py:333
  10.6 0.0 collective-permute-done.1.ry
  10.6 0.0 collective-permute-done.rx
  10.6 1.5 %early_forward.1 = (f32[16,256,256]{2,1,0:T(8,128)S(1)}, f32[16,256,256]{2,1,0:T(8,128)S(1)}, f32[16,256]{1,0:T(8,128)S(1)}, f32[16,256]{1,0:T(8,128)S(1)}, f32[...) custom-call(bf16[16,256,128]{2,1,0:T(8,128)(2,1)S(1)} %get-tuple-element.38.q, ...), custom_call_target="tpu_custom_call" | custom-call | flops 1000000000 | bytes 1048576 | tf_op jit(solution)/shard_map/early_forward/pallas_call | solution.py:333
  12.1 0.0 collective-permute-done.2.rz
  12.1 2.8 %late_pass.1 = (bf16[16,2,384,128]{3,2,1,0:T(8,128)(2,1)S(1)}, bf16[16,2,384,128]{3,2,1,0:T(8,128)(2,1)S(1)}, f32[16,256]{1,0:T(8,128)S(1)}, f32[16,256]{1,0:T(8...) custom-call(bf16[16,256,128]{2,1,0:T(8,128)(2,1)S(1)} %get-tuple-ele, ...), custom_call_target="tpu_custom_call" | custom-call | flops 1000000000 | bytes 1048576 | tf_op jit(solution)/shard_map/late_pass/pallas_call | solution.py:333
  14.9 1.2 %collective-permute-start.3 = (bf16[2,128,256]{2,1,0:T(8,128)(2,1)S(1)}, bf16[2,128,256]{2,1,0:T(8,128)(2,1)S(1)}, u32[]{:S(2)}, u32[]{:S(2)}) collective-permute-start(bf16[2,128,256]{2,1,0:T(8,128)(2,1)S(1)} %get-tuple-element.65), channel_id=1, source_target_pairs={{0,64},{1,65},{2,66},{3,67},{4,68},{5,69},{6,70},{7,71},{8,72},{9,... | collective-permute-start | bytes 393224 | tf_op jit(solution)/shard_map/ppermute | solution.py:358
  16.1 2.3 %collective-permute-start.4 = (bf16[2,128,256]{2,1,0:T(8,128)(2,1)S(1)}, bf16[2,128,256]{2,1,0:T(8,128)(2,1)S(1)}, u32[]{:S(2)}, u32[]{:S(2)}) collective-permute-start(bf16[2,128,256]{2,1,0:T(8,128)(2,1)S(1)} %get-tuple-element.66), channel_id=1, source_target_pairs={{0,192},{1,193},{2,194},{3,195},{4,196},{5,197},{6,198},{7,199},{8... | collective-permute-start | bytes 393224 | tf_op jit(solution)/shard_map/ppermute | solution.py:358
  18.4 1.4 %collective-permute-start.5 = (bf16[2,128,256]{2,1,0:T(8,128)(2,1)S(1)}, bf16[2,128,256]{2,1,0:T(8,128)(2,1)S(1)}, u32[]{:S(2)}, u32[]{:S(2)}) collective-permute-start(bf16[2,128,256]{2,1,0:T(8,128)(2,1)S(1)} %get-tuple-element.67), channel_id=1, source_target_pairs={{0,128},{1,129},{2,130},{3,131},{4,132},{5,133},{6,134},{7,135},{8... | collective-permute-start | bytes 393224 | tf_op jit(solution)/shard_map/ppermute | solution.py:358
  19.8 4.6 %local_backward.1 = (bf16[256,2048]{1,0:T(8,128)(2,1)}, bf16[256,2048]{1,0:T(8,128)(2,1)}, bf16[256,256]{1,0:T(8,128)(2,1)}, bf16[256,256]{1,0:T(8,128)(2,1)}, bf16[2,128,256]{2,1,0:T(8,128)(2,1)S(1)}) custom-call(bf16[16,256,128]{2,1,0:T(8,128)(2,1)S(1)} %get-tuple-element.38.q, bf16[16,256,128]{2,1,0:T(8,128)(2,1)S(1)} %get-tuple-element.39.do, ...), custom_call_target="tpu_custom_call" | custom-call | flops 1000000 | bytes 1048576 | tf_op jit(solution)/shard_map/local_backward/pallas_call | solution.py:333
  24.3 0.0 collective-permute-done.3.b
  24.3 0.0 collective-permute-done.4.c
  24.4 0.7 %collective-permute-done.5.d = bf16[2,128,256]{2,1,0:T(8,128)(2,1)S(1)} collective-permute-done((bf16[2,128,256]{2,1,0:T(8,128)(2,1)S(1)}, bf16[2,128,256]{2,1,0:T(8,128)(2,1)S(1)}, u32[]{:S(2)}, u32[]{:S(2)}) %collective-permute-start.5) | collective-permute-done | bytes 131104 | tf_op jit(solution)/shard_map/ppermute | solution.py:358
  25.1 0.7 %add_partials.1 = (bf16[128,256]{1,0:T(8,128)(2,1)}, bf16[128,256]{1,0:T(8,128)(2,1)}) custom-call(bf16[2,128,256]{2,1,0:T(8,128)(2,1)S(1)} %get-tuple-element.64.a, bf16[2,128,256]{2,1,0:T(8,128)(2,1)S(1)} %collective-permute-done.3.b, bf16[2,128,256]{2,1,0:T(8,128)(2,1)S(1)} %collective-permute-done.4.c, bf16[2,128,256]{2,1,0:T(8,128)(2,1)S(1)} %collective-permute-done.5.d), custom_call_target="tpu_custom_call" | custom-call | bytes 1048576 | tf_op jit(solution)/shard_map/add_partials/pallas_call | solution.py:333
Async XLA Ops:
  1.5 9.0 %collective-permute-start.1 = (bf16[2,128,256]{2,1,0:T(8,128)(2,1)S(1)}, bf16[2,128,256]{2,1,0:T(8,128)(2,1)S(1)}, u32[]{:S(2)}, u32[]{:S(2)}) collective-permute-start(bf16[2,128,256]{2,1,0:T(8,128)(2,1)S(1)} %pad_maximum_fusion), channel_id=1, source_target_pairs={{0,64},{1,65},{2,66},{3,67},{4,68},{5,69},{6,70},{7,71},{8,72},{9,... | collective-permute-start | bytes 393224 | tf_op jit(solution)/shard_map/ppermute | solution.py:358
  3.2 7.4 %collective-permute-start = (bf16[2,128,256]{2,1,0:T(8,128)(2,1)S(1)}, bf16[2,128,256]{2,1,0:T(8,128)(2,1)S(1)}, u32[]{:S(2)}, u32[]{:S(2)}) collective-permute-start(bf16[2,128,256]{2,1,0:T(8,128)(2,1)S(1)} %pad_maximum_fusion), channel_id=1, source_target_pairs={{0,192},{1,193},{2,194},{3,195},{4,196},{5,197},{6,198},{7,199},{8... | collective-permute-start | bytes 393224 | tf_op jit(solution)/shard_map/ppermute | solution.py:358
  4.8 7.3 %collective-permute-start.2 = (bf16[2,128,256]{2,1,0:T(8,128)(2,1)S(1)}, bf16[2,128,256]{2,1,0:T(8,128)(2,1)S(1)}, u32[]{:S(2)}, u32[]{:S(2)}) collective-permute-start(bf16[2,128,256]{2,1,0:T(8,128)(2,1)S(1)} %pad_maximum_fusion), channel_id=1, source_target_pairs={{0,128},{1,129},{2,130},{3,131},{4,132},{5,133},{6,134},{7,135},{8... | collective-permute-start | bytes 393224 | tf_op jit(solution)/shard_map/ppermute | solution.py:358
  14.9 9.5 %collective-permute-start.3 = (bf16[2,128,256]{2,1,0:T(8,128)(2,1)S(1)}, bf16[2,128,256]{2,1,0:T(8,128)(2,1)S(1)}, u32[]{:S(2)}, u32[]{:S(2)}) collective-permute-start(bf16[2,128,256]{2,1,0:T(8,128)(2,1)S(1)} %get-tuple-element.65), channel_id=1, source_target_pairs={{0,64},{1,65},{2,66},{3,67},{4,68},{5,69},{6,70},{7,71},{8,72},{9,... | collective-permute-start | bytes 393224 | tf_op jit(solution)/shard_map/ppermute | solution.py:358
  16.1 8.3 %collective-permute-start.4 = (bf16[2,128,256]{2,1,0:T(8,128)(2,1)S(1)}, bf16[2,128,256]{2,1,0:T(8,128)(2,1)S(1)}, u32[]{:S(2)}, u32[]{:S(2)}) collective-permute-start(bf16[2,128,256]{2,1,0:T(8,128)(2,1)S(1)} %get-tuple-element.66), channel_id=1, source_target_pairs={{0,192},{1,193},{2,194},{3,195},{4,196},{5,197},{6,198},{7,199},{8... | collective-permute-start | bytes 393224 | tf_op jit(solution)/shard_map/ppermute | solution.py:358
  18.4 6.7 %collective-permute-start.5 = (bf16[2,128,256]{2,1,0:T(8,128)(2,1)S(1)}, bf16[2,128,256]{2,1,0:T(8,128)(2,1)S(1)}, u32[]{:S(2)}, u32[]{:S(2)}) collective-permute-start(bf16[2,128,256]{2,1,0:T(8,128)(2,1)S(1)} %get-tuple-element.67), channel_id=1, source_target_pairs={{0,128},{1,129},{2,130},{3,131},{4,132},{5,133},{6,134},{7,135},{8... | collective-permute-start | bytes 393224 | tf_op jit(solution)/shard_map/ppermute | solution.py:358

commit v5 on v4

--- a/solution.py
+++ b/solution.py
@@ -19,7 +19,7 @@
 SCALE = HEAD_DIM**-0.5
 EXP2_SCALE = SCALE * 1.4426950408889634
 NEG = -1e30
-LOAD_AT = (0, 4)
+LOAD_AT = (0, 6)
 LATE_SKEW = 2
 F32 = jnp.float32
 BF16 = jnp.bfloat16

time: 26 us -> 26 us (level)
  no operation moved by 1% of the time
where the time goes in v5:
time: 26 us; the launch traced here: 25.8 us
  Pallas kernels  13.3 us (51%)
  starting transfers between devices  10.1 us (39%)
  other arithmetic  0.89 us (3%)
  waiting for transfers between devices  0.72 us (3%)
  between operations  0.7 us (3%)
    pallas_call x5, Pallas kernels, call(): pl.pallas_call(body, name=name, in_specs=[pl.BlockSpec(memory_space=in_sp...  13.3 us
    ppermute x6, starting transfers between devices, moved(): return lax.ppermute(block, 'rows', route)  10.1 us
    another operation x1, other arithmetic, per_device(): stacked = jnp.stack([prompt_keys, prompt_values])  0.89 us
    ppermute x6, waiting for transfers between devices, moved(): return lax.ppermute(block, 'rows', route)  0.72 us
  transfers between devices with their start and end apart: 6, of which 1 were waited for; matrix products, arithmetic and copies ran while one was open for 0% of the time, Pallas kernels for 38%

profile of v5, /device:TPU:96, one launch (start us, length us, event | category | flops | bytes accessed | tf_op | source)
XLA Modules:
  0.0 25.8 jit_solution(7468276332410946417)
XLA Ops:
  0.6 0.9 %pad_maximum_fusion = bf16[2,128,256]{2,1,0:T(8,128)(2,1)S(1)} fusion(bf16[1,128,256]{2,1,0:T(8,128)(2,1)} %bitcast.5, bf16[1,128,256]{2,1,0:T(8,128)(2,1)} %bitcast.4), kind=kLoop, calls=%fused_computation | loop fusion | flops 65536 | bytes 262144 | tf_op jit(solution)/shard_map/stack | solution.py:354
  1.5 1.7 %collective-permute-start.1 = (bf16[2,128,256]{2,1,0:T(8,128)(2,1)S(1)}, bf16[2,128,256]{2,1,0:T(8,128)(2,1)S(1)}, u32[]{:S(2)}, u32[]{:S(2)}) collective-permute-start(bf16[2,128,256]{2,1,0:T(8,128)(2,1)S(1)} %pad_maximum_fusion), channel_id=1, source_target_pairs={{0,64},{1,65},{2,66},{3,67},{4,68},{5,69},{6,70},{7,71},{8,72},{9,... | collective-permute-start | bytes 393224 | tf_op jit(solution)/shard_map/ppermute | solution.py:358
  3.2 1.7 %collective-permute-start = (bf16[2,128,256]{2,1,0:T(8,128)(2,1)S(1)}, bf16[2,128,256]{2,1,0:T(8,128)(2,1)S(1)}, u32[]{:S(2)}, u32[]{:S(2)}) collective-permute-start(bf16[2,128,256]{2,1,0:T(8,128)(2,1)S(1)} %pad_maximum_fusion), channel_id=1, source_target_pairs={{0,192},{1,193},{2,194},{3,195},{4,196},{5,197},{6,198},{7,199},{8... | collective-permute-start | bytes 393224 | tf_op jit(solution)/shard_map/ppermute | solution.py:358
  4.8 2.0 %collective-permute-start.2 = (bf16[2,128,256]{2,1,0:T(8,128)(2,1)S(1)}, bf16[2,128,256]{2,1,0:T(8,128)(2,1)S(1)}, u32[]{:S(2)}, u32[]{:S(2)}) collective-permute-start(bf16[2,128,256]{2,1,0:T(8,128)(2,1)S(1)} %pad_maximum_fusion), channel_id=1, source_target_pairs={{0,128},{1,129},{2,130},{3,131},{4,132},{5,133},{6,134},{7,135},{8... | collective-permute-start | bytes 393224 | tf_op jit(solution)/shard_map/ppermute | solution.py:358
  6.8 3.8 %local_forward.1 = (bf16[16,256,128]{2,1,0:T(8,128)(2,1)S(1)}, bf16[16,256,128]{2,1,0:T(8,128)(2,1)S(1)}, bf16[2,2,384,128]{3,2,1,0:T(8,128)(2,1)S(1)}, f32[16,2...) custom-call(bf16[256,2048]{1,0:T(8,128)(2,1)} %q_in.1, ...), custom_call_target="tpu_custom_call" | custom-call | flops 1000000000 | bytes 1048576 | tf_op jit(solution)/shard_map/local_forward/pallas_call | solution.py:333
  10.6 0.0 collective-permute-done.1.ry
  10.6 0.0 collective-permute-done.rx
  10.7 1.5 %early_forward.1 = (f32[16,256,256]{2,1,0:T(8,128)S(1)}, f32[16,256,256]{2,1,0:T(8,128)S(1)}, f32[16,256]{1,0:T(8,128)S(1)}, f32[16,256]{1,0:T(8,128)S(1)}, f32[...) custom-call(bf16[16,256,128]{2,1,0:T(8,128)(2,1)S(1)} %get-tuple-element.38.q, ...), custom_call_target="tpu_custom_call" | custom-call | flops 1000000000 | bytes 1048576 | tf_op jit(solution)/shard_map/early_forward/pallas_call | solution.py:333
  12.2 0.0 collective-permute-done.2.rz
  12.2 2.8 %late_pass.1 = (bf16[16,2,384,128]{3,2,1,0:T(8,128)(2,1)S(1)}, bf16[16,2,384,128]{3,2,1,0:T(8,128)(2,1)S(1)}, f32[16,256]{1,0:T(8,128)S(1)}, f32[16,256]{1,0:T(8...) custom-call(bf16[16,256,128]{2,1,0:T(8,128)(2,1)S(1)} %get-tuple-ele, ...), custom_call_target="tpu_custom_call" | custom-call | flops 1000000000 | bytes 1048576 | tf_op jit(solution)/shard_map/late_pass/pallas_call | solution.py:333
  14.9 1.1 %collective-permute-start.3 = (bf16[2,128,256]{2,1,0:T(8,128)(2,1)S(1)}, bf16[2,128,256]{2,1,0:T(8,128)(2,1)S(1)}, u32[]{:S(2)}, u32[]{:S(2)}) collective-permute-start(bf16[2,128,256]{2,1,0:T(8,128)(2,1)S(1)} %get-tuple-element.65), channel_id=1, source_target_pairs={{0,64},{1,65},{2,66},{3,67},{4,68},{5,69},{6,70},{7,71},{8,72},{9,... | collective-permute-start | bytes 393224 | tf_op jit(solution)/shard_map/ppermute | solution.py:358
  16.1 2.3 %collective-permute-start.4 = (bf16[2,128,256]{2,1,0:T(8,128)(2,1)S(1)}, bf16[2,128,256]{2,1,0:T(8,128)(2,1)S(1)}, u32[]{:S(2)}, u32[]{:S(2)}) collective-permute-start(bf16[2,128,256]{2,1,0:T(8,128)(2,1)S(1)} %get-tuple-element.66), channel_id=1, source_target_pairs={{0,192},{1,193},{2,194},{3,195},{4,196},{5,197},{6,198},{7,199},{8... | collective-permute-start | bytes 393224 | tf_op jit(solution)/shard_map/ppermute | solution.py:358
  18.4 1.4 %collective-permute-start.5 = (bf16[2,128,256]{2,1,0:T(8,128)(2,1)S(1)}, bf16[2,128,256]{2,1,0:T(8,128)(2,1)S(1)}, u32[]{:S(2)}, u32[]{:S(2)}) collective-permute-start(bf16[2,128,256]{2,1,0:T(8,128)(2,1)S(1)} %get-tuple-element.67), channel_id=1, source_target_pairs={{0,128},{1,129},{2,130},{3,131},{4,132},{5,133},{6,134},{7,135},{8... | collective-permute-start | bytes 393224 | tf_op jit(solution)/shard_map/ppermute | solution.py:358
  19.8 4.6 %local_backward.1 = (bf16[256,2048]{1,0:T(8,128)(2,1)}, bf16[256,2048]{1,0:T(8,128)(2,1)}, bf16[256,256]{1,0:T(8,128)(2,1)}, bf16[256,256]{1,0:T(8,128)(2,1)}, bf16[2,128,256]{2,1,0:T(8,128)(2,1)S(1)}) custom-call(bf16[16,256,128]{2,1,0:T(8,128)(2,1)S(1)} %get-tuple-element.38.q, bf16[16,256,128]{2,1,0:T(8,128)(2,1)S(1)} %get-tuple-element.39.do, ...), custom_call_target="tpu_custom_call" | custom-call | flops 1000000 | bytes 1048576 | tf_op jit(solution)/shard_map/local_backward/pallas_call | solution.py:333
  24.3 0.0 collective-permute-done.3.b
  24.3 0.0 collective-permute-done.4.c
  24.4 0.7 %collective-permute-done.5.d = bf16[2,128,256]{2,1,0:T(8,128)(2,1)S(1)} collective-permute-done((bf16[2,128,256]{2,1,0:T(8,128)(2,1)S(1)}, bf16[2,128,256]{2,1,0:T(8,128)(2,1)S(1)}, u32[]{:S(2)}, u32[]{:S(2)}) %collective-permute-start.5) | collective-permute-done | bytes 131104 | tf_op jit(solution)/shard_map/ppermute | solution.py:358
  25.1 0.7 %add_partials.1 = (bf16[128,256]{1,0:T(8,128)(2,1)}, bf16[128,256]{1,0:T(8,128)(2,1)}) custom-call(bf16[2,128,256]{2,1,0:T(8,128)(2,1)S(1)} %get-tuple-element.64.a, bf16[2,128,256]{2,1,0:T(8,128)(2,1)S(1)} %collective-permute-done.3.b, bf16[2,128,256]{2,1,0:T(8,128)(2,1)S(1)} %collective-permute-done.4.c, bf16[2,128,256]{2,1,0:T(8,128)(2,1)S(1)} %collective-permute-done.5.d), custom_call_target="tpu_custom_call" | custom-call | bytes 1048576 | tf_op jit(solution)/shard_map/add_partials/pallas_call | solution.py:333
Async XLA Ops:
  1.5 9.1 %collective-permute-start.1 = (bf16[2,128,256]{2,1,0:T(8,128)(2,1)S(1)}, bf16[2,128,256]{2,1,0:T(8,128)(2,1)S(1)}, u32[]{:S(2)}, u32[]{:S(2)}) collective-permute-start(bf16[2,128,256]{2,1,0:T(8,128)(2,1)S(1)} %pad_maximum_fusion), channel_id=1, source_target_pairs={{0,64},{1,65},{2,66},{3,67},{4,68},{5,69},{6,70},{7,71},{8,72},{9,... | collective-permute-start | bytes 393224 | tf_op jit(solution)/shard_map/ppermute | solution.py:358
  3.2 7.5 %collective-permute-start = (bf16[2,128,256]{2,1,0:T(8,128)(2,1)S(1)}, bf16[2,128,256]{2,1,0:T(8,128)(2,1)S(1)}, u32[]{:S(2)}, u32[]{:S(2)}) collective-permute-start(bf16[2,128,256]{2,1,0:T(8,128)(2,1)S(1)} %pad_maximum_fusion), channel_id=1, source_target_pairs={{0,192},{1,193},{2,194},{3,195},{4,196},{5,197},{6,198},{7,199},{8... | collective-permute-start | bytes 393224 | tf_op jit(solution)/shard_map/ppermute | solution.py:358
  4.8 7.3 %collective-permute-start.2 = (bf16[2,128,256]{2,1,0:T(8,128)(2,1)S(1)}, bf16[2,128,256]{2,1,0:T(8,128)(2,1)S(1)}, u32[]{:S(2)}, u32[]{:S(2)}) collective-permute-start(bf16[2,128,256]{2,1,0:T(8,128)(2,1)S(1)} %pad_maximum_fusion), channel_id=1, source_target_pairs={{0,128},{1,129},{2,130},{3,131},{4,132},{5,133},{6,134},{7,135},{8... | collective-permute-start | bytes 393224 | tf_op jit(solution)/shard_map/ppermute | solution.py:358
  14.9 9.4 %collective-permute-start.3 = (bf16[2,128,256]{2,1,0:T(8,128)(2,1)S(1)}, bf16[2,128,256]{2,1,0:T(8,128)(2,1)S(1)}, u32[]{:S(2)}, u32[]{:S(2)}) collective-permute-start(bf16[2,128,256]{2,1,0:T(8,128)(2,1)S(1)} %get-tuple-element.65), channel_id=1, source_target_pairs={{0,64},{1,65},{2,66},{3,67},{4,68},{5,69},{6,70},{7,71},{8,72},{9,... | collective-permute-start | bytes 393224 | tf_op jit(solution)/shard_map/ppermute | solution.py:358
  16.1 8.3 %collective-permute-start.4 = (bf16[2,128,256]{2,1,0:T(8,128)(2,1)S(1)}, bf16[2,128,256]{2,1,0:T(8,128)(2,1)S(1)}, u32[]{:S(2)}, u32[]{:S(2)}) collective-permute-start(bf16[2,128,256]{2,1,0:T(8,128)(2,1)S(1)} %get-tuple-element.66), channel_id=1, source_target_pairs={{0,192},{1,193},{2,194},{3,195},{4,196},{5,197},{6,198},{7,199},{8... | collective-permute-start | bytes 393224 | tf_op jit(solution)/shard_map/ppermute | solution.py:358
  18.4 6.7 %collective-permute-start.5 = (bf16[2,128,256]{2,1,0:T(8,128)(2,1)S(1)}, bf16[2,128,256]{2,1,0:T(8,128)(2,1)S(1)}, u32[]{:S(2)}, u32[]{:S(2)}) collective-permute-start(bf16[2,128,256]{2,1,0:T(8,128)(2,1)S(1)} %get-tuple-element.67), channel_id=1, source_target_pairs={{0,128},{1,129},{2,130},{3,131},{4,132},{5,133},{6,134},{7,135},{8... | collective-permute-start | bytes 393224 | tf_op jit(solution)/shard_map/ppermute | solution.py:358
